TPU v7x, 1024 devices: a whole 8x8x8 slice. The times are simulated.
1024 devices in a mesh: modes: 128 (over z, y, core), grid: 8 (over x).
Axes of the slice: x: 8, y: 8, z: 8, core: 2. Of those that a mesh axis runs over, the one named last changes fastest.
Arguments:
- u_modes: float32 [128, 2, 64, 1024], P('modes', None, 'grid'), may hold values from -5 to 5
- v_modes: float32 [128, 2, 64, 1024], P('modes', None, 'grid'), may hold values from -0.85 to 0.85
- potential: float32 [64, 1024], P('grid'), may hold values from -1.5 to 0
- pairing: float32 [2, 64, 1024], P(None, 'grid'), may hold values from -1 to 1
Outputs:
- u_next: float32 [128, 2, 64, 1024], P('modes', None, 'grid')
- v_next: float32 [128, 2, 64, 1024], P('modes', None, 'grid')
- fields: float32 [4, 64, 1024], P(None, 'grid')
All inputs are finite; a program needn't handle non-finite values.
Results may differ from a plain program's by a relative error of at most 0.00035.
Values sent between devices are 32-bit elements; how exact they have to be, the bound alone decides.
A program may use at most 64 MiB of HBM per device.

v0:
```python
import jax
import jax.numpy as jnp
from jax import lax
from jax.sharding import PartitionSpec as P

NX = 32
NY = 32


stencil_coef = (-205.0 / 72.0, 8.0 / 5.0, -1.0 / 5.0, 8.0 / 315.0, -1.0 / 560.0)
alpha_coef = 1.14
beta_coef = -0.553
gamma_coef = -11.11
time_step = 0.18
epsilon = 1e-06


def extended(x, sides, width):
    for axis, dim in sides:
        count, length = (lax.axis_size(axis), x.shape[dim])
        up = [(i, (i + 1) % count) for i in range(count)]
        down = [(j, i) for i, j in up]
        last = lax.slice_in_dim(x, length - width, length, axis=dim)
        leading = lax.slice_in_dim(x, 0, width, axis=dim)
        before = lax.ppermute(last, axis, up)
        after = lax.ppermute(leading, axis, down)
        x = jnp.concatenate([before, x, after], axis=dim)
    return x


def laplace_plane(region):
    shaped = region.reshape(region.shape[:3] + (NY, NX))
    total = 2.0 * stencil_coef[0] * shaped
    for offset in range(1, 5):
        total = total + stencil_coef[offset] * (
            jnp.roll(shaped, offset, 3)
            + jnp.roll(shaped, -offset, 3)
            + jnp.roll(shaped, offset, 4)
            + jnp.roll(shaped, -offset, 4)
        )
    return total.reshape(region.shape)


def laplace_depth(wide, start, count):
    total = stencil_coef[0] * wide[:, :, start : start + count]
    for offset in range(1, 5):
        total = total + stencil_coef[offset] * (
            wide[:, :, start + offset : start + offset + count]
            + wide[:, :, start - offset : start - offset + count]
        )
    return total


def laplace(states):
    planes = states.shape[2]
    padded = extended(states, (("grid", 2),), 4)
    return laplace_depth(padded, 4, planes) + laplace_plane(states)


def laplace_first(states):
    planes = states.shape[2]
    padded = extended(states, (("grid", 2),), 4)
    return laplace_depth(padded, 4, planes) + laplace_plane(states)


def slopes(states, laplace_now, field_pot, pair_re, pair_im):
    kinetic = -0.5 * alpha_coef * laplace_now + field_pot * states
    upper_re = kinetic[:, 0] + pair_re * states[:, 2] - pair_im * states[:, 3]
    upper_im = kinetic[:, 1] + pair_re * states[:, 3] + pair_im * states[:, 2]
    lower_re = pair_re * states[:, 0] + pair_im * states[:, 1] - kinetic[:, 2]
    lower_im = pair_re * states[:, 1] - pair_im * states[:, 0] - kinetic[:, 3]
    return jnp.stack([upper_im, -upper_re, lower_im, -lower_re], axis=1)


def potentials(raw_sums, modes_total):
    density = 2.0 * raw_sums[0] / modes_total
    kinetic = -2.0 * raw_sums[1] / modes_total
    anomal_re = raw_sums[2] / modes_total
    anomal_im = raw_sums[3] / modes_total
    dense_safe = density + epsilon
    fermi = 0.5 * jnp.power(3.0 * jnp.pi**2 * dense_safe, 2.0 / 3.0)
    anomal_sq = anomal_re * anomal_re + anomal_im * anomal_im
    third_root = jnp.power(dense_safe, -1.0 / 3.0)
    field_pot = beta_coef * fermi - gamma_coef / 3.0 * anomal_sq * third_root / dense_safe
    pair_re = -gamma_coef * anomal_re * third_root
    pair_im = -gamma_coef * anomal_im * third_root
    energy = (
        alpha_coef * kinetic / 2.0
        + 0.6 * beta_coef * dense_safe * fermi
        + gamma_coef * anomal_sq * third_root
    )
    return jnp.stack([field_pot, pair_re, pair_im, energy], axis=0)


def local(u_modes, v_modes, potential, pairing):
    start_state = jnp.concatenate([u_modes, v_modes], axis=1)

    def slope_at(states):
        return slopes(states, laplace_first(states), potential, pairing[0], pairing[1])

    slope_one = slope_at(start_state)
    slope_two = slope_at(start_state + 0.5 * time_step * slope_one)
    slope_three = slope_at(start_state + 0.5 * time_step * slope_two)
    slope_four = slope_at(start_state + time_step * slope_three)
    stepped = start_state + time_step / 6.0 * (
        slope_one + 2.0 * slope_two + 2.0 * slope_three + slope_four
    )
    lap_step = laplace(stepped)
    partial_sums = jnp.stack(
        [
            jnp.sum(stepped[:, 2] * stepped[:, 2] + stepped[:, 3] * stepped[:, 3], axis=0),
            jnp.sum(stepped[:, 2] * lap_step[:, 2] + stepped[:, 3] * lap_step[:, 3], axis=0),
            jnp.sum(stepped[:, 0] * stepped[:, 2] + stepped[:, 1] * stepped[:, 3], axis=0),
            jnp.sum(stepped[:, 1] * stepped[:, 2] - stepped[:, 0] * stepped[:, 3], axis=0),
        ],
        axis=0,
    )
    modes_total = float(stepped.shape[0] * lax.axis_size("modes"))
    raw_sums = lax.psum(partial_sums, "modes")
    fields = potentials(raw_sums, modes_total)
    next_one = slopes(stepped, lap_step, fields[0], fields[1], fields[2])
    middle = stepped + 0.5 * time_step * next_one
    next_two = slopes(middle, laplace(middle), fields[0], fields[1], fields[2])
    result = stepped + time_step / 6.0 * (next_one + 2.0 * next_two)
    return (result[:, 0:2], result[:, 2:4], fields)


def solution(mesh):
    placed = (
        P("modes", None, "grid", None),
        P("modes", None, "grid", None),
        P("grid", None),
        P(None, "grid", None),
    )
    return jax.shard_map(
        local,
        mesh=mesh,
        in_specs=placed,
        out_specs=(
            P("modes", None, "grid", None),
            P("modes", None, "grid", None),
            P(None, "grid", None),
        ),
        check_vma=False,
    )
```

profile of v0, /device:TPU:1, one launch (start us, length us, event | category | flops | bytes accessed | tf_op | source)
XLA Modules:
  0.0 426.1 jit_solution(6295964439600138102)
XLA Ops:
  8.8 5.3 %collective-permute-start = (f32[1,4,4,1024]{3,2,1,0:T(4,128)}, f32[1,4,4,1024]{3,2,1,0:T(4,128)}, u32[]{:S(2)}, u32[]{:S(2)}) collective-permute-start(f32[1,4,4,1024]{3,2,1,0:T(4,128)} %get-tuple-element.239), channel_id=1, source_target_pairs={{1,0},{2,1},{3,2},{4,3},{5,4},{6,5},{7,6},{0,7},{9,8},{10,9},{11,1... | collective-permute-start | bytes 196616 | tf_op jit(solution)/shard_map/ppermute | solution.py:26
  14.1 1.9 collective-permute-start.1
  16.2 1.2 fusion.348
  17.4 1.2 fusion.349
  23.3 1.2 fusion.357
  31.5 2.2 fusion.2
  34.5 1.4 fusion.5
  37.0 2.2 fusion.8
  40.3 1.4 fusion.11
  43.7 1.5 fusion.175
  49.9 1.2 fusion.340
  55.0 1.2 fusion.345
  59.3 1.7 fusion.17
  62.1 2.1 fusion.20
  66.5 4.6 %collective-permute-start.2 = (f32[1,4,4,1024]{3,2,1,0:T(4,128)}, f32[1,4,4,1024]{3,2,1,0:T(4,128)}, u32[]{:S(2)}, u32[]{:S(2)}) collective-permute-start(f32[1,4,4,1024]{3,2,1,0:T(4,128)} %get-tuple-element.237), channel_id=1, source_target_pairs={{1,0},{2,1},{3,2},{4,3},{5,4},{6,5},{7,6},{0,7},{9,8},{10,9},{11,1... | collective-permute-start | bytes 196616 | tf_op jit(solution)/shard_map/ppermute | solution.py:26
  71.1 2.1 collective-permute-start.3
  73.3 1.7 fusion.23
  75.3 2.1 collective-permute-done.3
  77.4 1.4 fusion.156
  86.9 1.2 fusion.328
  92.3 1.9 fusion.29
  95.2 2.0 fusion.32
  99.7 3.1 collective-permute-start.4
  102.8 2.1 collective-permute-start.5
  105.0 1.9 fusion.35
  107.2 2.2 collective-permute-done.5
  109.4 1.4 fusion.137
  112.8 1.2 fusion.305
  120.9 1.2 fusion.313
  125.1 2.1 fusion.41
  128.1 2.2 fusion.44
  131.9 2.9 collective-permute-start.6
  134.8 2.6 collective-permute-start.7
  137.4 2.0 fusion.47
  141.4 1.5 fusion.118
  156.1 1.6 fusion.55
  158.8 2.1 fusion.58
  162.0 3.4 collective-permute-start.8
  165.4 2.3 collective-permute-start.9
  167.7 1.6 fusion.61
  169.7 2.0 collective-permute-done.9
  172.7 209.4 %all-reduce.2.cloned.1.call-done = f32[4,8,1024]{2,1,0:T(8,128)} async-done(((f32[4,8,1024]{2,1,0:T(8,128)}), f32[4,8,1024]{2,1,0:T(8,128)}) %all-reduce.2.cloned.1.call-update) | async-done | bytes 131088 | tf_op jit(solution)/shard_map/psum | solution.py:119
  398.9 1.4 fusion.68
  401.3 2.2 fusion.71
  404.6 1.4 fusion.74
  407.1 4.5 %collective-permute-start.10 = (f32[1,4,4,1024]{3,2,1,0:T(4,128)S(1)}, f32[1,4,4,1024]{3,2,1,0:T(4,128)S(1)}, u32[]{:S(2)}, u32[]{:S(2)}) collective-permute-start(f32[1,4,4,1024]{3,2,1,0:T(4,128)S(1)} %get-tuple-element.225), channel_id=1, source_target_pairs={{1,0},{2,1},{3,2},{4,3},{5,4},{6,5},{7,6},{0,7},{9,8},{10,9},{11,1... | collective-permute-start | bytes 196616 | tf_op jit(solution)/shard_map/ppermute | solution.py:26
  411.6 1.9 collective-permute-start.11
  414.2 3.9 collective-permute-done.11
  (440 shorter events, 103.6 us)
Async XLA Ops:
  7.2 374.9 %all-reduce.2.cloned.1.call-start = ((), (), s32[]{:S(2)}) async-start(), calls=%async_computation | async-start | bytes 262144 | tf_op jit(solution)/shard_map/psum | solution.py:119
  8.8 34.0 %collective-permute-start = (f32[1,4,4,1024]{3,2,1,0:T(4,128)}, f32[1,4,4,1024]{3,2,1,0:T(4,128)}, u32[]{:S(2)}, u32[]{:S(2)}) collective-permute-start(f32[1,4,4,1024]{3,2,1,0:T(4,128)} %get-tuple-element.239), channel_id=1, source_target_pairs={{1,0},{2,1},{3,2},{4,3},{5,4},{6,5},{7,6},{0,7},{9,8},{10,9},{11,1... | collective-permute-start | bytes 196616 | tf_op jit(solution)/shard_map/ppermute | solution.py:26
  14.1 28.7 %collective-permute-start.1 = (f32[1,4,4,1024]{3,2,1,0:T(4,128)}, f32[1,4,4,1024]{3,2,1,0:T(4,128)}, u32[]{:S(2)}, u32[]{:S(2)}) collective-permute-start(f32[1,4,4,1024]{3,2,1,0:T(4,128)} %get-tuple-element.240), channel_id=1, source_target_pairs={{0,1},{1,2},{2,3},{3,4},{4,5},{5,6},{6,7},{7,0},{8,9},{9,10},{10,1... | collective-permute-start | bytes 196616 | tf_op jit(solution)/shard_map/ppermute | solution.py:25
  46.0 19.0 %copy-start.36 = (f32[1,8,1024]{2,1,0:T(8,128)}, f32[1,8,1024]{2,1,0:T(8,128)S(1)}, u32[]{:S(2)}) copy-start(f32[1,8,1024]{2,1,0:T(8,128)S(1)} %get-tuple-element.214) | copy-start | bytes 98308
  46.0 19.0 %copy-start.39 = (f32[1,8,1024]{2,1,0:T(8,128)}, f32[1,8,1024]{2,1,0:T(8,128)S(1)}, u32[]{:S(2)}) copy-start(f32[1,8,1024]{2,1,0:T(8,128)S(1)} %get-tuple-element.215) | copy-start | bytes 98308
  62.1 11.2 %copy-start.6 = (f32[1,4,8,32,4]{4,3,2,1,0:T(8,128)S(1)}, f32[1,4,8,32,4]{4,3,2,1,0:T(8,128)}, u32[]{:S(2)}) copy-start(f32[1,4,8,32,4]{4,3,2,1,0:T(8,128)} %get-tuple-element.160) | copy-start | bytes 49156
  64.1 9.1 %copy-start.1 = (f32[1,4,8,32,28]{4,3,2,1,0:T(8,128)S(1)}, f32[1,4,8,32,28]{4,3,2,1,0:T(8,128)}, u32[]{:S(2)}) copy-start(f32[1,4,8,32,28]{4,3,2,1,0:T(8,128)} %get-tuple-element.158) | copy-start | bytes 344068
  64.2 9.1 %copy-start.2 = (f32[1,4,8,32,28]{4,3,2,1,0:T(8,128)S(1)}, f32[1,4,8,32,28]{4,3,2,1,0:T(8,128)}, u32[]{:S(2)}) copy-start(f32[1,4,8,32,28]{4,3,2,1,0:T(8,128)} %get-tuple-element.159) | copy-start | bytes 344068
  65.9 7.4 %copy-start.109 = (f32[1,4,8,4,32]{4,3,2,1,0:T(4,128)S(1)}, f32[1,4,8,4,32]{4,3,2,1,0:T(4,128)}, u32[]{:S(2)}) copy-start(f32[1,4,8,4,32]{4,3,2,1,0:T(4,128)} %get-tuple-element.164) | copy-start | bytes 49156
  65.9 7.4 %copy-start.110 = (f32[1,4,8,4,32]{4,3,2,1,0:T(4,128)S(1)}, f32[1,4,8,4,32]{4,3,2,1,0:T(4,128)}, u32[]{:S(2)}) copy-start(f32[1,4,8,4,32]{4,3,2,1,0:T(4,128)} %get-tuple-element.165) | copy-start | bytes 49156
  66.5 8.7 %collective-permute-start.2 = (f32[1,4,4,1024]{3,2,1,0:T(4,128)}, f32[1,4,4,1024]{3,2,1,0:T(4,128)}, u32[]{:S(2)}, u32[]{:S(2)}) collective-permute-start(f32[1,4,4,1024]{3,2,1,0:T(4,128)} %get-tuple-element.237), channel_id=1, source_target_pairs={{1,0},{2,1},{3,2},{4,3},{5,4},{6,5},{7,6},{0,7},{9,8},{10,9},{11,1... | collective-permute-start | bytes 196616 | tf_op jit(solution)/shard_map/ppermute | solution.py:26
  71.1 6.3 %collective-permute-start.3 = (f32[1,4,4,1024]{3,2,1,0:T(4,128)S(1)}, f32[1,4,4,1024]{3,2,1,0:T(4,128)}, u32[]{:S(2)}, u32[]{:S(2)}) collective-permute-start(f32[1,4,4,1024]{3,2,1,0:T(4,128)S(1)} %get-tuple-element.238), channel_id=1, source_target_pairs={{0,1},{1,2},{2,3},{3,4},{4,5},{5,6},{6,7},{7,0},{8,9},{9,10},{10,1... | collective-permute-start | bytes 196616 | tf_op jit(solution)/shard_map/ppermute | solution.py:25
  97.3 7.7 %copy-start.3 = (f32[1,4,8,32,28]{4,3,2,1,0:T(8,128)S(1)}, f32[1,4,8,32,28]{4,3,2,1,0:T(8,128)}, u32[]{:S(2)}) copy-start(f32[1,4,8,32,28]{4,3,2,1,0:T(8,128)} %get-tuple-element.126) | copy-start | bytes 344068
  97.3 7.7 %copy-start.4 = (f32[1,4,8,32,28]{4,3,2,1,0:T(8,128)S(1)}, f32[1,4,8,32,28]{4,3,2,1,0:T(8,128)}, u32[]{:S(2)}) copy-start(f32[1,4,8,32,28]{4,3,2,1,0:T(8,128)} %get-tuple-element.127) | copy-start | bytes 344068
  99.0 6.0 %copy-start.111 = (f32[1,4,8,4,32]{4,3,2,1,0:T(4,128)S(1)}, f32[1,4,8,4,32]{4,3,2,1,0:T(4,128)}, u32[]{:S(2)}) copy-start(f32[1,4,8,4,32]{4,3,2,1,0:T(4,128)} %get-tuple-element.132) | copy-start | bytes 49156
  99.0 6.0 %copy-start.112 = (f32[1,4,8,4,32]{4,3,2,1,0:T(4,128)S(1)}, f32[1,4,8,4,32]{4,3,2,1,0:T(4,128)}, u32[]{:S(2)}) copy-start(f32[1,4,8,4,32]{4,3,2,1,0:T(4,128)} %get-tuple-element.133) | copy-start | bytes 49156
  99.7 7.5 %collective-permute-start.4 = (f32[1,4,4,1024]{3,2,1,0:T(4,128)}, f32[1,4,4,1024]{3,2,1,0:T(4,128)}, u32[]{:S(2)}, u32[]{:S(2)}) collective-permute-start(f32[1,4,4,1024]{3,2,1,0:T(4,128)} %get-tuple-element.235), channel_id=1, source_target_pairs={{1,0},{2,1},{3,2},{4,3},{5,4},{6,5},{7,6},{0,7},{9,8},{10,9},{11,1... | collective-permute-start | bytes 196616 | tf_op jit(solution)/shard_map/ppermute | solution.py:26
  102.8 6.5 %collective-permute-start.5 = (f32[1,4,4,1024]{3,2,1,0:T(4,128)}, f32[1,4,4,1024]{3,2,1,0:T(4,128)}, u32[]{:S(2)}, u32[]{:S(2)}) collective-permute-start(f32[1,4,4,1024]{3,2,1,0:T(4,128)} %get-tuple-element.236), channel_id=1, source_target_pairs={{0,1},{1,2},{2,3},{3,4},{4,5},{5,6},{6,7},{7,0},{8,9},{9,10},{10,1... | collective-permute-start | bytes 196616 | tf_op jit(solution)/shard_map/ppermute | solution.py:25
  110.8 20.4 %copy-start.30 = (f32[1,8,1024]{2,1,0:T(8,128)}, f32[1,8,1024]{2,1,0:T(8,128)S(1)}, u32[]{:S(2)}) copy-start(f32[1,8,1024]{2,1,0:T(8,128)S(1)} %get-tuple-element.210) | copy-start | bytes 98308
  110.8 20.4 %copy-start.33 = (f32[1,8,1024]{2,1,0:T(8,128)}, f32[1,8,1024]{2,1,0:T(8,128)S(1)}, u32[]{:S(2)}) copy-start(f32[1,8,1024]{2,1,0:T(8,128)S(1)} %fusion.243) | copy-start | bytes 98308
  131.2 6.2 %copy-start.5 = (f32[1,4,8,32,28]{4,3,2,1,0:T(8,128)S(1)}, f32[1,4,8,32,28]{4,3,2,1,0:T(8,128)}, u32[]{:S(2)}) copy-start(f32[1,4,8,32,28]{4,3,2,1,0:T(8,128)} %get-tuple-element.94) | copy-start | bytes 344068
  131.2 6.2 %copy-start.113 = (f32[1,4,8,4,32]{4,3,2,1,0:T(4,128)S(1)}, f32[1,4,8,4,32]{4,3,2,1,0:T(4,128)}, u32[]{:S(2)}) copy-start(f32[1,4,8,4,32]{4,3,2,1,0:T(4,128)} %get-tuple-element.100) | copy-start | bytes 49156
  131.2 6.2 %copy-start.114 = (f32[1,4,8,4,32]{4,3,2,1,0:T(4,128)S(1)}, f32[1,4,8,4,32]{4,3,2,1,0:T(4,128)}, u32[]{:S(2)}) copy-start(f32[1,4,8,4,32]{4,3,2,1,0:T(4,128)} %get-tuple-element.101) | copy-start | bytes 49156
  131.9 8.5 %collective-permute-start.6 = (f32[1,4,4,1024]{3,2,1,0:T(4,128)}, f32[1,4,4,1024]{3,2,1,0:T(4,128)}, u32[]{:S(2)}, u32[]{:S(2)}) collective-permute-start(f32[1,4,4,1024]{3,2,1,0:T(4,128)} %get-tuple-element.233), channel_id=1, source_target_pairs={{1,0},{2,1},{3,2},{4,3},{5,4},{6,5},{7,6},{0,7},{9,8},{10,9},{11,1... | collective-permute-start | bytes 196616 | tf_op jit(solution)/shard_map/ppermute | solution.py:26
  134.8 6.5 %collective-permute-start.7 = (f32[1,4,4,1024]{3,2,1,0:T(4,128)}, f32[1,4,4,1024]{3,2,1,0:T(4,128)}, u32[]{:S(2)}, u32[]{:S(2)}) collective-permute-start(f32[1,4,4,1024]{3,2,1,0:T(4,128)} %get-tuple-element.234), channel_id=1, source_target_pairs={{0,1},{1,2},{2,3},{3,4},{4,5},{5,6},{6,7},{7,0},{8,9},{9,10},{10,1... | collective-permute-start | bytes 196616 | tf_op jit(solution)/shard_map/ppermute | solution.py:25
  158.8 9.0 %copy-start.10 = (f32[1,4,8,32,4]{4,3,2,1,0:T(8,128)S(1)}, f32[1,4,8,32,4]{4,3,2,1,0:T(8,128)}, u32[]{:S(2)}) copy-start(f32[1,4,8,32,4]{4,3,2,1,0:T(8,128)} %get-tuple-element.65) | copy-start | bytes 49156
  160.9 6.8 %copy-start.9 = (f32[1,4,8,32,4]{4,3,2,1,0:T(8,128)S(1)}, f32[1,4,8,32,4]{4,3,2,1,0:T(8,128)}, u32[]{:S(2)}) copy-start(f32[1,4,8,32,4]{4,3,2,1,0:T(8,128)} %get-tuple-element.64) | copy-start | bytes 49156
  161.9 5.8 %copy-start.7 = (f32[1,4,8,32,28]{4,3,2,1,0:T(8,128)S(1)}, f32[1,4,8,32,28]{4,3,2,1,0:T(8,128)}, u32[]{:S(2)}) copy-start(f32[1,4,8,32,28]{4,3,2,1,0:T(8,128)} %get-tuple-element.62) | copy-start | bytes 344068
  161.9 5.8 %copy-start.8 = (f32[1,4,8,32,28]{4,3,2,1,0:T(8,128)S(1)}, f32[1,4,8,32,28]{4,3,2,1,0:T(8,128)}, u32[]{:S(2)}) copy-start(f32[1,4,8,32,28]{4,3,2,1,0:T(8,128)} %get-tuple-element.63) | copy-start | bytes 344068
  162.0 7.7 %collective-permute-start.8 = (f32[1,4,4,1024]{3,2,1,0:T(4,128)S(1)}, f32[1,4,4,1024]{3,2,1,0:T(4,128)S(1)}, u32[]{:S(2)}, u32[]{:S(2)}) collective-permute-start(f32[1,4,4,1024]{3,2,1,0:T(4,128)S(1)} %get-tuple-element.231), channel_id=1, source_target_pairs={{1,0},{2,1},{3,2},{4,3},{5,4},{6,5},{7,6},{0,7},{9,8},{10,9},{11,1... | collective-permute-start | bytes 196616 | tf_op jit(solution)/shard_map/ppermute | solution.py:26
  165.4 6.2 %collective-permute-start.9 = (f32[1,4,4,1024]{3,2,1,0:T(4,128)S(1)}, f32[1,4,4,1024]{3,2,1,0:T(4,128)S(1)}, u32[]{:S(2)}, u32[]{:S(2)}) collective-permute-start(f32[1,4,4,1024]{3,2,1,0:T(4,128)S(1)} %get-tuple-element.232), channel_id=1, source_target_pairs={{0,1},{1,2},{2,3},{3,4},{4,5},{5,6},{6,7},{7,0},{8,9},{9,10},{10,1... | collective-permute-start | bytes 196616 | tf_op jit(solution)/shard_map/ppermute | solution.py:25
  172.6 211.0 %copy-start.52 = (f32[1,8,1024]{2,1,0:T(8,128)S(1)}, f32[1,8,1024]{2,1,0:T(8,128)}, u32[]{:S(2)}) copy-start(f32[1,8,1024]{2,1,0:T(8,128)} %copy-done.50) | copy-start | bytes 98308
  172.6 211.0 %copy-start.56 = (f32[1,8,1024]{2,1,0:T(8,128)S(1)}, f32[1,8,1024]{2,1,0:T(8,128)}, u32[]{:S(2)}) copy-start(f32[1,8,1024]{2,1,0:T(8,128)} %copy-done.54) | copy-start | bytes 98308
  172.6 211.0 %copy-start.60 = (f32[1,8,1024]{2,1,0:T(8,128)S(1)}, f32[1,8,1024]{2,1,0:T(8,128)}, u32[]{:S(2)}) copy-start(f32[1,8,1024]{2,1,0:T(8,128)} %copy-done.58) | copy-start | bytes 98308
  172.6 211.0 %copy-start.64 = (f32[1,8,1024]{2,1,0:T(8,128)S(1)}, f32[1,8,1024]{2,1,0:T(8,128)}, u32[]{:S(2)}) copy-start(f32[1,8,1024]{2,1,0:T(8,128)} %copy-done.62) | copy-start | bytes 98308
  172.7 210.9 %copy-start.38 = (f32[1,8,1024]{2,1,0:T(8,128)S(1)}, f32[1,8,1024]{2,1,0:T(8,128)}, u32[]{:S(2)}) copy-start(f32[1,8,1024]{2,1,0:T(8,128)} %copy-done.36) | copy-start | bytes 98308
  172.7 210.9 %copy-start.41 = (f32[1,8,1024]{2,1,0:T(8,128)S(1)}, f32[1,8,1024]{2,1,0:T(8,128)}, u32[]{:S(2)}) copy-start(f32[1,8,1024]{2,1,0:T(8,128)} %copy-done.39) | copy-start | bytes 98308
  172.7 210.9 %copy-start.44 = (f32[1,8,1024]{2,1,0:T(8,128)S(1)}, f32[1,8,1024]{2,1,0:T(8,128)}, u32[]{:S(2)}) copy-start(f32[1,8,1024]{2,1,0:T(8,128)} %copy-done.42) | copy-start | bytes 98308
  172.7 210.9 %copy-start.48 = (f32[1,8,1024]{2,1,0:T(8,128)S(1)}, f32[1,8,1024]{2,1,0:T(8,128)}, u32[]{:S(2)}) copy-start(f32[1,8,1024]{2,1,0:T(8,128)} %copy-done.46) | copy-start | bytes 98308
  407.0 6.5 %copy-start.118 = (f32[1,8,1024]{2,1,0:T(8,128)S(1)}, f32[1,8,1024]{2,1,0:T(8,128)}, u32[]{:S(2)}) copy-start(f32[1,8,1024]{2,1,0:T(8,128)} %get-tuple-element.219) | copy-start | bytes 98308
  407.0 6.5 %copy-start.84 = (f32[1,8,1024]{2,1,0:T(8,128)S(1)}, f32[1,8,1024]{2,1,0:T(8,128)}, u32[]{:S(2)}) copy-start(f32[1,8,1024]{2,1,0:T(8,128)} %copy-done.83) | copy-start | bytes 98308
  407.0 6.5 %copy-start.86 = (f32[1,8,1024]{2,1,0:T(8,128)S(1)}, f32[1,8,1024]{2,1,0:T(8,128)}, u32[]{:S(2)}) copy-start(f32[1,8,1024]{2,1,0:T(8,128)} %copy-done.85) | copy-start | bytes 98308
  407.0 6.5 %copy-start.117 = (f32[1,8,1024]{2,1,0:T(8,128)S(1)}, f32[1,8,1024]{2,1,0:T(8,128)}, u32[]{:S(2)}) copy-start(f32[1,8,1024]{2,1,0:T(8,128)} %get-tuple-element.218) | copy-start | bytes 98308
  407.0 11.1 %copy-start.97 = (f32[1,4,8,1024]{3,2,1,0:T(8,128)S(1)}, f32[1,4,8,1024]{3,2,1,0:T(8,128)}, u32[]{:S(2)}) copy-start(f32[1,4,8,1024]{3,2,1,0:T(8,128)} %mul.1635) | copy-start | bytes 393220
  407.1 11.1 %copy-start.108 = (f32[8,1024]{1,0:T(8,128)S(1)}, f32[8,1024]{1,0:T(8,128)}, u32[]{:S(2)}) copy-start(f32[8,1024]{1,0:T(8,128)} %copy-done.107) | copy-start | bytes 98308
  407.1 7.1 %collective-permute-start.10 = (f32[1,4,4,1024]{3,2,1,0:T(4,128)S(1)}, f32[1,4,4,1024]{3,2,1,0:T(4,128)S(1)}, u32[]{:S(2)}, u32[]{:S(2)}) collective-permute-start(f32[1,4,4,1024]{3,2,1,0:T(4,128)S(1)} %get-tuple-element.225), channel_id=1, source_target_pairs={{1,0},{2,1},{3,2},{4,3},{5,4},{6,5},{7,6},{0,7},{9,8},{10,9},{11,1... | collective-permute-start | bytes 196616 | tf_op jit(solution)/shard_map/ppermute | solution.py:26
  411.6 6.6 %collective-permute-start.11 = (f32[1,4,4,1024]{3,2,1,0:T(4,128)S(1)}, f32[1,4,4,1024]{3,2,1,0:T(4,128)S(1)}, u32[]{:S(2)}, u32[]{:S(2)}) collective-permute-start(f32[1,4,4,1024]{3,2,1,0:T(4,128)S(1)} %get-tuple-element.226), channel_id=1, source_target_pairs={{0,1},{1,2},{2,3},{3,4},{4,5},{5,6},{6,7},{7,0},{8,9},{9,10},{10,1... | collective-permute-start | bytes 196616 | tf_op jit(solution)/shard_map/ppermute | solution.py:25
  413.5 4.6 %copy-start.87 = (f32[1,4,8,1024]{3,2,1,0:T(8,128)S(1)}, f32[1,4,8,1024]{3,2,1,0:T(8,128)}, u32[]{:S(2)}) copy-start(f32[1,4,8,1024]{3,2,1,0:T(8,128)} %mul.1631) | copy-start | bytes 393220
  (84 other events, 136.0 us)
Sparse Core Ops, SparseCore 0:
  172.8 209.2 all-reduce.1
where the time goes:
time: 428 us; the launch traced here: 426 us
  waiting for transfers between devices  221 us (52%)
  local copies, waits for them, and re-layouts  103 us (24%)
  other arithmetic  49.4 us (12%)
  starting transfers between devices  36.8 us (9%)
  between operations  15.8 us (4%)
    psum x1, waiting for transfers between devices, local(): raw_sums = lax.psum(partial_sums, 'modes')  209 us
    slice x48, local copies, waits for them, and re-layouts, laplace_plane(): jnp.roll(shaped, -offset, 4)  37.9 us
    mul x24, other arithmetic, laplace_plane(): stencil_coef[offset]  37.6 us
    slice x48, local copies, waits for them, and re-layouts, laplace_plane(): jnp.roll(shaped, -offset, 3)  31.1 us
    ppermute x6, starting transfers between devices, extended(): after = lax.ppermute(leading, axis, down)  23.8 us
    mul x24, local copies, waits for them, and re-layouts, laplace_plane(): stencil_coef[offset]  18 us
    ppermute x6, starting transfers between devices, extended(): before = lax.ppermute(last, axis, up)  12.9 us
    ppermute x6, waiting for transfers between devices, extended(): before = lax.ppermute(last, axis, up)  11.1 us
  transfers between devices with their start and end apart: 13, of which 6 were waited for; matrix products, arithmetic and copies ran while one was open for 8% of the time, Pallas kernels for 0%

commit v1 on v0

v1 whole, which is shorter than its diff:
```python
import functools
import math

import jax
import jax.numpy as jnp
from jax import lax
from jax.experimental import pallas as pl
from jax.experimental.pallas import tpu as pltpu
from jax.sharding import PartitionSpec as P

MESH = pl.DeviceIdType.MESH
COEF = (-205.0 / 72.0, 8.0 / 5.0, -1.0 / 5.0, 8.0 / 315.0, -1.0 / 560.0)
ALPHA = 1.14
BETA = -0.553
GAMMA = -11.11
DT = 0.18
EPS = 1e-06
PLANES = 8
ROWS = 8
LANES = 128


def in_plane(x, masks):
    lane32, lane, _ = masks
    total = (3.0 * COEF[0]) * x

    def turn(shift):
        return pltpu.roll(x, shift, 2)

    for k in range(1, 5):
        minus = jnp.where(lane32 >= k, turn(k), turn(96 + k))
        plus = jnp.where(lane32 < 32 - k, turn(128 - k), turn(32 - k))
        total = total + COEF[k] * (minus + plus)
    zero = jnp.float32(0.0)
    up = COEF[4] * x
    down = up
    for j in range(1, 4):
        moved = turn(128 - 32 * j)
        near, far = COEF[j], COEF[4 - j]
        within = lane < 128 - 32 * j
        total = total + jnp.where(within, near, far) * moved
        up = up + jnp.where(within, zero, near) * moved
        down = down + jnp.where(within, far, zero) * moved
    return total + pltpu.roll(up, ROWS - 1, 1) + pltpu.roll(down, 1, 1)


def slope(x, lap, pot, pr, pi):
    kin = [(-0.5 * ALPHA) * lap[c] + pot * x[c] for c in range(4)]
    return [
        kin[1] + pr * x[3] + pi * x[2],
        pi * x[3] - pr * x[2] - kin[0],
        pr * x[1] - pi * x[0] - kin[3],
        kin[2] - pr * x[0] - pi * x[1],
    ]


def kernel(
    n,
    grid_n,
    modes_total,
    u_ref,
    v_ref,
    pot_ref,
    pair_ref,
    uo_ref,
    vo_ref,
    fo_ref,
    raw,
    rows,
    xs,
    pots,
    acc,
    base,
    lap1,
    q1,
    halo_lo,
    halo_hi,
    sums,
    pair_in,
    piece_in,
    gather_in,
    field_mine,
    field_other,
    load_sem,
    halo_send,
    halo_recv,
    pair_sem,
    first_send,
    first_recv,
    second_send,
    second_recv,
    back_send,
    back_recv,
):
    m = lax.axis_index("modes")
    g = lax.axis_index("grid")
    core = lax.rem(m, 2)
    yy = lax.rem(m // 2, n)
    zz = m // (2 * n)
    left = (m, lax.rem(g + grid_n - 1, grid_n))
    right = (m, lax.rem(g + 1, grid_n))
    sibling = (m + 1 - 2 * core, g)
    first = yy + core * (zz - yy)
    second = zz + core * (yy - zz)
    first_base = (1 - core) * zz * 2 * n + core * (yy * 2 + 1)
    first_step = 2 + core * (2 * n - 2)
    second_base = (1 - core) * yy * 2 + core * (zz * 2 * n + 1)
    second_step = 2 * n - core * (2 * n - 2)
    share = PLANES // n

    def first_peer(d):
        return (first_base + lax.rem(first + d, n) * first_step, g)

    def second_peer(d):
        return (second_base + lax.rem(second + d, n) * second_step, g)

    loads = [
        pltpu.make_async_copy(u_ref.at[0], raw.at[0:2], load_sem.at[0]),
        pltpu.make_async_copy(v_ref.at[0], raw.at[2:4], load_sem.at[1]),
        pltpu.make_async_copy(pot_ref, raw.at[4], load_sem.at[2]),
        pltpu.make_async_copy(pair_ref, raw.at[5:7], load_sem.at[3]),
    ]
    for load in loads:
        load.start()

    barrier = pltpu.get_barrier_semaphore()
    partners = [left, right, sibling]
    partners += [first_peer(d) for d in range(1, n)] + [second_peer(d) for d in range(1, n)]
    for partner in partners:
        pl.semaphore_signal(barrier, inc=1, device_id=partner, device_id_type=MESH)

    lane = lax.broadcasted_iota(jnp.int32, (1, ROWS, LANES), 2)
    row = lax.broadcasted_iota(jnp.int32, (ROWS, LANES), 0)
    masks = (lax.rem(lane, 32), lane, None)
    top = row < 4

    for load in loads:
        load.wait()
    for c in range(7):
        for t in range(ROWS):
            rows[c, t * PLANES : (t + 1) * PLANES, :] = raw[c, :, t * LANES : (t + 1) * LANES]
    for c in range(7):
        for z in range(PLANES):
            plane = rows[c, pl.ds(z, ROWS, stride=PLANES), :]
            if c < 4:
                xs[0, z, c] = plane
                acc[z, c] = plane
            else:
                pots[z, c - 4] = plane
    pl.semaphore_wait(barrier, len(partners))

    def to_left(s):
        return pltpu.make_async_remote_copy(
            src_ref=xs.at[s, 0:4],
            dst_ref=halo_hi.at[s],
            send_sem=halo_send.at[0, s],
            recv_sem=halo_recv.at[1, s],
            device_id=left,
            device_id_type=MESH,
        )

    def to_right(s):
        return pltpu.make_async_remote_copy(
            src_ref=xs.at[s, 4:8],
            dst_ref=halo_lo.at[s],
            send_sem=halo_send.at[1, s],
            recv_sem=halo_recv.at[0, s],
            device_id=right,
            device_id_type=MESH,
        )

    def own_part(s):
        def plane_part(z, carry):
            base[z] = in_plane(xs[s, z], masks)
            return carry

        lax.fori_loop(0, PLANES, plane_part, 0)
        for z in range(PLANES):
            total = base[z]
            for k in range(1, 5):
                if z - k >= 0 and z + k < PLANES:
                    total = total + COEF[k] * (xs[s, z - k] + xs[s, z + k])
                elif z - k >= 0:
                    total = total + COEF[k] * xs[s, z - k]
                elif z + k < PLANES:
                    total = total + COEF[k] * xs[s, z + k]
            base[z] = total

    def with_halo(s, z):
        total = base[z]
        for k in range(1, 5):
            if z - k < 0:
                total = total + COEF[k] * halo_lo[s, 4 + z - k]
            if z + k >= PLANES:
                total = total + COEF[k] * halo_hi[s, z + k - PLANES]
        return total

    to_left(0).start()
    to_right(0).start()

    def stage(s, carry):
        own_part(s)
        last = s == 3
        reach = jnp.where(s == 2, DT, 0.5 * DT).astype(jnp.float32)
        weight = jnp.where((s == 0) | last, DT / 6.0, DT / 3.0).astype(jnp.float32)
        for side in (0, 1):
            (to_right if side == 0 else to_left)(s).wait_recv()
            for z in range(4 * side, 4 * side + 4):
                x = xs[s, z]
                k = slope(x, with_halo(s, z), pots[z, 0], pots[z, 1], pots[z, 2])
                for c in range(4):
                    total = acc[z, c] + weight * k[c]
                    acc[z, c] = total
                    xs[s + 1, z, c] = jnp.where(last, total, xs[0, z, c] + reach * k[c])
            (to_left if side == 0 else to_right)(s + 1).start()
        return carry

    lax.fori_loop(0, 4, stage, 0)

    own_part(4)
    for side in (0, 1):
        (to_right if side == 0 else to_left)(4).wait_recv()
        for z in range(4 * side, 4 * side + 4):
            x = xs[4, z]
            lap = with_halo(4, z)
            lap1[z] = lap
            four = [
                x[2] * x[2] + x[3] * x[3],
                x[2] * lap[2] + x[3] * lap[3],
                x[0] * x[2] + x[1] * x[3],
                x[1] * x[2] - x[0] * x[3],
            ]
            for p in range(2):
                a, b = four[2 * p], four[2 * p + 1]
                sums[0, z, p] = jnp.where(top, a, pltpu.roll(b, 4, 0))
                sums[1, z, p] = jnp.where(top, pltpu.roll(a, 4, 0), b)
    pair_copy = pltpu.make_async_remote_copy(
        src_ref=sums.at[1 - core],
        dst_ref=pair_in,
        send_sem=pair_sem.at[0],
        recv_sem=pair_sem.at[1],
        device_id=sibling,
        device_id_type=MESH,
    )
    pair_copy.start()
    pair_copy.wait_recv()
    pair_in[...] = pair_in[...] + sums[core]

    order = sorted(range(1, n), key=lambda d: -min(d, n - d))
    first_copies = []
    for d in order:
        copy = pltpu.make_async_remote_copy(
            src_ref=pair_in.at[pl.ds(lax.rem(first + d, n) * share, share)],
            dst_ref=piece_in.at[d - 1],
            send_sem=first_send.at[d - 1],
            recv_sem=first_recv.at[d - 1],
            device_id=first_peer(d),
            device_id_type=MESH,
        )
        copy.start()
        first_copies.append(copy)
    total = pair_in[pl.ds(first * share, share)]
    for copy in reversed(first_copies):
        copy.wait_recv()
    for d in range(1, n):
        total = total + piece_in[d - 1]
    gather_in[0] = total

    second_copies = []
    for d in order:
        copy = pltpu.make_async_remote_copy(
            src_ref=gather_in.at[0],
            dst_ref=gather_in.at[d],
            send_sem=second_send.at[d - 1],
            recv_sem=second_recv.at[d - 1],
            device_id=second_peer(d),
            device_id_type=MESH,
        )
        copy.start()
        second_copies.append(copy)
    for copy in reversed(second_copies):
        copy.wait_recv()
    total = gather_in[second]
    for i in range(1, n):
        total = total + gather_in[lax.rem(second + n - i, n)]

    for z in range(share):
        s01, s23 = total[z, 0], total[z, 1]
        density = (2.0 / modes_total) * s01
        kinetic = (-2.0 / modes_total) * pltpu.roll(s01, 4, 0)
        an_re = (1.0 / modes_total) * s23
        an_im = (1.0 / modes_total) * pltpu.roll(s23, 4, 0)
        dense = jnp.where(top, density, jnp.float32(1.0)) + EPS
        third_root = jnp.exp(jnp.log(dense) * (-1.0 / 3.0))
        fermi = (0.5 * (3.0 * math.pi**2) ** (2.0 / 3.0)) * (dense * third_root)
        an_sq = an_re * an_re + an_im * an_im
        f0 = BETA * fermi - (GAMMA / 3.0) * an_sq * third_root / dense
        f1 = -GAMMA * an_re * third_root
        f2 = -GAMMA * an_im * third_root
        f3 = (0.5 * ALPHA) * kinetic + (0.6 * BETA) * dense * fermi + GAMMA * an_sq * third_root
        field_mine[0, z, 0] = jnp.where(top, f0, pltpu.roll(f1, 4, 0))
        field_mine[0, z, 1] = jnp.where(top, f2, pltpu.roll(f3, 4, 0))

    back_copies = []
    for d in order:
        copy = pltpu.make_async_remote_copy(
            src_ref=field_mine.at[0],
            dst_ref=field_mine.at[d],
            send_sem=back_send.at[d - 1],
            recv_sem=back_recv.at[d - 1],
            device_id=first_peer(d),
            device_id_type=MESH,
        )
        copy.start()
        back_copies.append(copy)
    for copy in reversed(back_copies):
        copy.wait_recv()
    pair_back = pltpu.make_async_remote_copy(
        src_ref=field_mine,
        dst_ref=field_other,
        send_sem=pair_sem.at[2],
        recv_sem=pair_sem.at[3],
        device_id=sibling,
        device_id_type=MESH,
    )
    pair_back.start()
    pair_back.wait_recv()

    even = core == 0
    for z in range(PLANES):
        place, part = z // share, z % share
        mine = field_mine[lax.rem(first + n - place, n), part]
        other = field_other[lax.rem(second + n - place, n), part]
        fields = []
        for p in range(2):
            low = jnp.where(even, mine[p], other[p])
            high = jnp.where(even, other[p], mine[p])
            fields.append(jnp.where(top, low, pltpu.roll(high, 4, 0)))
            fields.append(jnp.where(top, pltpu.roll(low, 4, 0), high))
        for c in range(3):
            pots[z, c] = fields[c]
        for c in range(4):
            rows[c, z * ROWS : (z + 1) * ROWS, :] = fields[c]
        x = xs[4, z]
        k = slope(x, lap1[z], fields[0], fields[1], fields[2])
        for c in range(4):
            q1[z, c] = k[c]
            xs[5, z, c] = x[c] + (0.5 * DT) * k[c]
        if z == 3:
            to_left(5).start()
    to_right(5).start()
    for c in range(4):
        for t in range(ROWS):
            fo_ref[c, :, t * LANES : (t + 1) * LANES] = rows[c, pl.ds(t, PLANES, stride=ROWS), :]
    own_part(5)
    for side in (0, 1):
        (to_right if side == 0 else to_left)(5).wait_recv()
        for z in range(4 * side, 4 * side + 4):
            k = slope(xs[5, z], with_halo(5, z), pots[z, 0], pots[z, 1], pots[z, 2])
            for c in range(4):
                out = xs[4, z, c] + (DT / 6.0) * (q1[z, c] + 2.0 * k[c])
                rows[c, z * ROWS : (z + 1) * ROWS, :] = out
    for c in range(4):
        for t in range(ROWS):
            block = rows[c, pl.ds(t, PLANES, stride=ROWS), :]
            if c < 2:
                uo_ref[0, c, :, t * LANES : (t + 1) * LANES] = block
            else:
                vo_ref[0, c - 2, :, t * LANES : (t + 1) * LANES] = block

    for s in range(6):
        to_left(s).wait_send()
        to_right(s).wait_send()
    pair_copy.wait_send()
    pair_back.wait_send()
    for copy in first_copies + second_copies + back_copies:
        copy.wait_send()


def solution(mesh):
    modes, grid_n = mesh.shape["modes"], mesh.shape["grid"]
    n = math.isqrt(modes // 2)
    share = PLANES // n
    f32 = jnp.float32
    plane = (ROWS, LANES)

    def local(u_modes, v_modes, potential, pairing):
        vmem = pl.BlockSpec(memory_space=pltpu.VMEM)
        return pl.pallas_call(
            functools.partial(kernel, n, grid_n, float(modes)),
            out_shape=(
                jax.ShapeDtypeStruct(u_modes.shape, f32),
                jax.ShapeDtypeStruct(v_modes.shape, f32),
                jax.ShapeDtypeStruct((4,) + potential.shape, f32),
            ),
            in_specs=[pl.BlockSpec(memory_space=pl.ANY)] * 4,
            out_specs=(vmem, vmem, vmem),
            scratch_shapes=[
                pltpu.VMEM((7, PLANES, ROWS * LANES), f32),
                pltpu.VMEM((7, PLANES * ROWS, LANES), f32),
                pltpu.VMEM((6, PLANES, 4) + plane, f32),
                pltpu.VMEM((PLANES, 3) + plane, f32),
                pltpu.VMEM((PLANES, 4) + plane, f32),
                pltpu.VMEM((PLANES, 4) + plane, f32),
                pltpu.VMEM((PLANES, 4) + plane, f32),
                pltpu.VMEM((PLANES, 4) + plane, f32),
                pltpu.VMEM((6, 4, 4) + plane, f32),
                pltpu.VMEM((6, 4, 4) + plane, f32),
                pltpu.VMEM((2, PLANES, 2) + plane, f32),
                pltpu.VMEM((PLANES, 2) + plane, f32),
                pltpu.VMEM((n - 1, share, 2) + plane, f32),
                pltpu.VMEM((n, share, 2) + plane, f32),
                pltpu.VMEM((n, share, 2) + plane, f32),
                pltpu.VMEM((n, share, 2) + plane, f32),
                pltpu.SemaphoreType.DMA((4,)),
                pltpu.SemaphoreType.DMA((2, 6)),
                pltpu.SemaphoreType.DMA((2, 6)),
                pltpu.SemaphoreType.DMA((4,)),
                pltpu.SemaphoreType.DMA((n - 1,)),
                pltpu.SemaphoreType.DMA((n - 1,)),
                pltpu.SemaphoreType.DMA((n - 1,)),
                pltpu.SemaphoreType.DMA((n - 1,)),
                pltpu.SemaphoreType.DMA((n - 1,)),
                pltpu.SemaphoreType.DMA((n - 1,)),
            ],
            compiler_params=pltpu.CompilerParams(
                collective_id=0, has_side_effects=True, vmem_limit_bytes=32 * 1024 * 1024
            ),
        )(u_modes, v_modes, potential, pairing)

    placed = (
        P("modes", None, "grid", None),
        P("modes", None, "grid", None),
        P("grid", None),
        P(None, "grid", None),
    )
    return jax.shard_map(
        local,
        mesh=mesh,
        in_specs=placed,
        out_specs=(placed[0], placed[1], placed[3]),
        check_vma=False,
    )
```

time: 428 us -> 67.7 us (0.16)
  waiting for transfers between devices: 221 us -> 0 us
  local copies, waits for them, and re-layouts: 103 us -> 5.18 us
  Pallas kernels: 0 us -> 61.6 us
  other arithmetic: 49.4 us -> 0 us
  starting transfers between devices: 36.8 us -> 0 us
  between operations: 15.8 us -> 0.65 us
    psum x1 -> x0, waiting for transfers between devices: 209 us -> none  [local(): raw_sums = lax.psum(partial_sums, 'modes')]
    slice x103 -> x0, local copies, waits for them, and re-layouts: 72.4 us -> none  [the longest x48 37.9 us: laplace_plane(): jnp.roll(shaped, -offset, 4)]
    pallas_call x0 -> x1, Pallas kernels: none -> 61.6 us  [local(): pl.pallas_call(functools.partial(kernel, n, grid_n, float(modes)), out_sh...]
    mul x24 -> x0, other arithmetic: 37.6 us -> none  [laplace_plane(): stencil_coef[offset]]
    ppermute x12 -> x0, starting transfers between devices: 36.7 us -> none  [the longest x6 23.8 us: extended(): after = lax.ppermute(leading, axis, down)]
    mul x24 -> x0, local copies, waits for them, and re-layouts: 18 us -> none  [laplace_plane(): stencil_coef[offset]]
    ppermute x12 -> x0, waiting for transfers between devices: 11.2 us -> none  [the longest x6 11.1 us: extended(): before = lax.ppermute(last, axis, up)]
    add x23 -> x0, other arithmetic: 8.83 us -> none  [the longest x6 6.02 us: slopes(): kinetic = -0.5 * alpha_coef * laplace_now + field_pot * states]
  transfers between devices with their start and end apart: 13 -> 0, of which waited for: 6 -> 0; matrix products, arithmetic and copies ran while one was open for 8% -> 0% of each run, Pallas kernels for 0% -> 0%
where the time goes in v1:
time: 67.7 us; the launch traced here: 67.4 us
  Pallas kernels  61.6 us (91%)
  local copies, waits for them, and re-layouts  5.18 us (8%)
    pallas_call x1, Pallas kernels, local(): pl.pallas_call(functools.partial(kernel, n, grid_n, float(modes)), out_sh...  61.6 us
    unnamed x11, local copies, waits for them, and re-layouts  5.18 us

profile of v1, /device:TPU:1, one launch (start us, length us, event | category | flops | bytes accessed | tf_op | source)
XLA Modules:
  0.0 67.4 jit_solution(7576760317350211380)
XLA Ops:
  0.6 0.0 copy-start
  0.6 0.8 %copy-done = f32[1,2,8,1024]{3,2,1,0:T(8,128)S(1)} copy-done((f32[1,2,8,1024]{3,2,1,0:T(8,128)S(1)}, f32[1,2,8,1024]{3,2,1,0:T(8,128)}, u32[]{:S(2)}) %copy-start) | copy-done | bytes 65560
  1.5 0.0 copy-start.1
  1.5 0.8 %copy-done.1 = f32[1,2,8,1024]{3,2,1,0:T(8,128)S(1)} copy-done((f32[1,2,8,1024]{3,2,1,0:T(8,128)S(1)}, f32[1,2,8,1024]{3,2,1,0:T(8,128)}, u32[]{:S(2)}) %copy-start.1) | copy-done | bytes 65560
  2.3 0.0 copy-start.2
  2.3 0.8 %copy-done.2 = f32[2,8,1024]{2,1,0:T(8,128)S(1)} copy-done((f32[2,8,1024]{2,1,0:T(8,128)S(1)}, f32[2,8,1024]{2,1,0:T(8,128)}, u32[]{:S(2)}) %copy-start.2) | copy-done | bytes 65560
  3.2 0.0 copy-start.3
  3.2 0.8 %copy-done.3 = f32[8,1024]{1,0:T(8,128)S(1)} copy-done((f32[8,1024]{1,0:T(8,128)S(1)}, f32[8,1024]{1,0:T(8,128)}, u32[]{:S(2)}) %copy-start.3) | copy-done | bytes 32792
  3.9 61.6 %shard_map.67 = (f32[1,2,8,1024]{3,2,1,0:T(8,128)S(1)}, f32[1,2,8,1024]{3,2,1,0:T(8,128)S(1)}, f32[4,8,1024]{2,1,0:T(8,128)S(1)}) custom-call(f32[1,2,8,1024]{3,2,1,0:T(8,128)S(1)} %copy-done, f32[1,2,8,1024]{3,2,1,0:T(8,128)S(1)} %copy-done.1, f32[8,1024]{1,0:T(8,128)S(1)} %copy-done.3, f32[2,8,1024]{2,1,0:T(8,128)S(1)} %copy-done.2), custom_call_target="tpu_custom_call" | custom-call | tf_op jit(solution)/shard_map/pallas_call | solution.py:389
  65.5 0.6 copy.10
  66.1 0.6 copy.11
  66.7 0.7 copy.12
Async XLA Ops:
  0.6 0.8 %copy-start = (f32[1,2,8,1024]{3,2,1,0:T(8,128)S(1)}, f32[1,2,8,1024]{3,2,1,0:T(8,128)}, u32[]{:S(2)}) copy-start(f32[1,2,8,1024]{3,2,1,0:T(8,128)} %u_ref.1) | copy-start | bytes 196612
  1.5 0.8 %copy-start.1 = (f32[1,2,8,1024]{3,2,1,0:T(8,128)S(1)}, f32[1,2,8,1024]{3,2,1,0:T(8,128)}, u32[]{:S(2)}) copy-start(f32[1,2,8,1024]{3,2,1,0:T(8,128)} %v_ref.1) | copy-start | bytes 196612
  2.3 0.8 %copy-start.2 = (f32[2,8,1024]{2,1,0:T(8,128)S(1)}, f32[2,8,1024]{2,1,0:T(8,128)}, u32[]{:S(2)}) copy-start(f32[2,8,1024]{2,1,0:T(8,128)} %pair_ref.1) | copy-start | bytes 196612
  3.2 0.8 %copy-start.3 = (f32[8,1024]{1,0:T(8,128)S(1)}, f32[8,1024]{1,0:T(8,128)}, u32[]{:S(2)}) copy-start(f32[8,1024]{1,0:T(8,128)} %pot_ref.1) | copy-start | bytes 98308

commit v2 on v1

v2 whole, which is shorter than its diff:
```python
import functools
import math

import jax
import jax.numpy as jnp
from jax import lax
from jax.experimental import pallas as pl
from jax.experimental.pallas import tpu as pltpu
from jax.sharding import PartitionSpec as P

MESH = pl.DeviceIdType.MESH
COEF = (-205.0 / 72.0, 8.0 / 5.0, -1.0 / 5.0, 8.0 / 315.0, -1.0 / 560.0)
ALPHA = 1.14
BETA = -0.553
GAMMA = -11.11
DT = 0.18
EPS = 1e-06
PLANES = 8
ROWS = 8
LANES = 128


def spread(weights):
    source = lax.broadcasted_iota(jnp.int32, (LANES, LANES), 0)
    target = lax.broadcasted_iota(jnp.int32, (LANES, LANES), 1)
    dx = lax.rem(lax.rem(source, 32) + 32 - lax.rem(target, 32), 32)
    dy = source // 32 - target // 32
    zero = jnp.zeros((LANES, LANES), jnp.float32)
    within, above, below = zero, zero, zero
    for k in range(1, 5):
        within = jnp.where((dy == 0) & ((dx == k) | (dx == 32 - k)), COEF[k], within)
        within = jnp.where((dx == 0) & ((dy == k) | (dy == -k)), COEF[k], within)
        above = jnp.where((dx == 0) & (dy + 4 == k), COEF[k], above)
        below = jnp.where((dx == 0) & (4 - dy == k), COEF[k], below)
    for i, part in enumerate((within, above, below)):
        high = part.astype(jnp.bfloat16)
        low = (part - high.astype(jnp.float32)).astype(jnp.bfloat16)
        for half in range(2):
            weights[i, LANES * half : LANES * (half + 1), 0:LANES] = high
            weights[i, LANES * half : LANES * (half + 1), LANES : 2 * LANES] = low


def in_plane(x, weights):
    flat = x.reshape(-1, LANES)
    high = flat.astype(jnp.bfloat16)
    low = (flat - high.astype(jnp.float32)).astype(jnp.bfloat16)
    both = jnp.concatenate([high, low], axis=1)

    def times(i):
        wide = jnp.dot(both, weights[i], preferred_element_type=jnp.float32)
        return (wide[:, :LANES] + wide[:, LANES:]).reshape(x.shape)

    return (3.0 * COEF[0]) * x + times(0) + pltpu.roll(times(1), ROWS - 1, 1) + pltpu.roll(times(2), 1, 1)


def slope(x, lap, pot, pr, pi):
    kin = [(-0.5 * ALPHA) * lap[c] + pot * x[c] for c in range(4)]
    return [
        kin[1] + pr * x[3] + pi * x[2],
        pi * x[3] - pr * x[2] - kin[0],
        pr * x[1] - pi * x[0] - kin[3],
        kin[2] - pr * x[0] - pi * x[1],
    ]


def turned(h):
    return [h[1], -h[0], -h[3], h[2]]


def kernel(
    n,
    grid_n,
    modes_total,
    u_ref,
    v_ref,
    pot_ref,
    pair_ref,
    out_rows,
    field_rows,
    raw,
    rows,
    xs,
    pots,
    acc,
    base,
    pre,
    halo_lo,
    halo_hi,
    sums,
    piece_in,
    gather_in,
    field_mine,
    field_other,
    weights,
    load_sem,
    halo_send,
    halo_recv,
    first_send,
    first_recv,
    second_send,
    second_recv,
    back_send,
    back_recv,
):
    m = lax.axis_index("modes")
    g = lax.axis_index("grid")
    core = lax.rem(m, 2)
    yy = lax.rem(m // 2, n)
    zz = m // (2 * n)
    left = (m, lax.rem(g + grid_n - 1, grid_n))
    right = (m, lax.rem(g + 1, grid_n))
    flip = 1 - 2 * core
    first = yy + core * (zz - yy)
    second = zz + core * (yy - zz)
    first_base = (1 - core) * zz * 2 * n + core * (yy * 2 + 1)
    first_step = 2 + core * (2 * n - 2)
    second_base = (1 - core) * yy * 2 + core * (zz * 2 * n + 1)
    second_step = 2 * n - core * (2 * n - 2)
    share = PLANES // n
    first_at = [lax.rem(first + d, n) for d in range(n)]
    second_at = [lax.rem(second + d, n) for d in range(n)]
    first_peer = [(first_base + at * first_step, g) for at in first_at]
    second_peer = [(second_base + at * second_step, g) for at in second_at]
    first_cross = [(peer[0] + flip, g) for peer in first_peer]
    second_cross = [(peer[0] + flip, g) for peer in second_peer]

    barrier = pltpu.get_barrier_semaphore()
    partners = [left, right] + first_cross + first_peer[1:] + second_peer[1:] + second_cross[1:]
    for partner in partners:
        pl.semaphore_signal(barrier, inc=1, device_id=partner, device_id_type=MESH)

    loads = [
        pltpu.make_async_copy(u_ref.at[0], raw.at[0:2], load_sem.at[0]),
        pltpu.make_async_copy(v_ref.at[0], raw.at[2:4], load_sem.at[1]),
        pltpu.make_async_copy(pot_ref, raw.at[4], load_sem.at[2]),
        pltpu.make_async_copy(pair_ref, raw.at[5:7], load_sem.at[3]),
    ]
    for load in loads:
        load.start()
    spread(weights)

    row = lax.broadcasted_iota(jnp.int32, (ROWS, LANES), 0)
    top = row < 4

    for load in loads:
        load.wait()
    for c in range(7):
        for t in range(ROWS):
            rows[c, t * PLANES : (t + 1) * PLANES, :] = raw[c, :, t * LANES : (t + 1) * LANES]
    for c in range(7):
        for z in range(PLANES):
            plane = rows[c, pl.ds(z, ROWS, stride=PLANES), :]
            if c < 4:
                xs[0, z, c] = plane
                acc[z, c] = plane
            else:
                pots[z, c - 4] = plane
    pl.semaphore_wait(barrier, len(partners))

    def to_left(s):
        return pltpu.make_async_remote_copy(
            src_ref=xs.at[s, 0:4],
            dst_ref=halo_hi.at[s],
            send_sem=halo_send.at[0, s],
            recv_sem=halo_recv.at[1, s],
            device_id=left,
            device_id_type=MESH,
        )

    def to_right(s):
        return pltpu.make_async_remote_copy(
            src_ref=xs.at[s, 4:8],
            dst_ref=halo_lo.at[s],
            send_sem=halo_send.at[1, s],
            recv_sem=halo_recv.at[0, s],
            device_id=right,
            device_id_type=MESH,
        )

    def own_plane(s):
        base[...] = in_plane(xs[s].reshape(PLANES * 4, ROWS, LANES), weights).reshape(base.shape)

    def own_part(s, z):
        total = base[z]
        for k in range(1, 5):
            if z - k >= 0 and z + k < PLANES:
                total = total + COEF[k] * (xs[s, z - k] + xs[s, z + k])
            elif z - k >= 0:
                total = total + COEF[k] * xs[s, z - k]
            elif z + k < PLANES:
                total = total + COEF[k] * xs[s, z + k]
        return total

    def halo_part(s, z, scale):
        parts = [(scale * COEF[k]) * halo_lo[s, 4 + z - k] for k in range(1, 5) if z - k < 0]
        parts += [(scale * COEF[k]) * halo_hi[s, z + k - PLANES] for k in range(1, 5) if z + k >= PLANES]
        return sum(parts[1:], parts[0])

    def arrived(s, side):
        (to_right if side == 0 else to_left)(s).wait_recv()
        return range(4 * side, 4 * side + 4)

    def send(s, side):
        (to_left if side == 0 else to_right)(s).start()

    send(0, 0)
    send(0, 1)

    def stage(s, carry):
        last = s == 3
        weight = jnp.where((s == 0) | last, DT / 6.0, DT / 3.0).astype(jnp.float32)
        reach = jnp.where(s == 2, DT, 0.5 * DT).astype(jnp.float32)
        after = jnp.where(last, weight, reach)
        own_plane(s)
        for z in range(PLANES):
            k = slope(xs[s, z], own_part(s, z), pots[z, 0], pots[z, 1], pots[z, 2])
            for c in range(4):
                total = acc[z, c] + weight * k[c]
                acc[z, c] = total
                pre[z, c] = jnp.where(last, total, xs[0, z, c] + reach * k[c])
        for side in (0, 1):
            more = {}
            for z in arrived(s, side):
                more[z] = turned(halo_part(s, z, -0.5 * ALPHA))
                for c in range(4):
                    xs[s + 1, z, c] = pre[z, c] + after * more[z][c]
            send(s + 1, side)
            for z in more:
                for c in range(4):
                    acc[z, c] = acc[z, c] + weight * more[z][c]
        return carry

    lax.fori_loop(0, 4, stage, 0)

    own_plane(4)
    for z in range(PLANES):
        base[z] = own_part(4, z)
        x = xs[4, z]
        an_re = x[0] * x[2] + x[1] * x[3]
        an_im = x[1] * x[2] - x[0] * x[3]
        sums[0, z, 1] = jnp.where(top, an_re, pltpu.roll(an_im, 4, 0))
        sums[1, z, 1] = jnp.where(top, pltpu.roll(an_re, 4, 0), an_im)
    for side in (0, 1):
        for z in arrived(4, side):
            x = xs[4, z]
            lap = base[z] + halo_part(4, z, 1.0)
            base[z] = lap
            dense = x[2] * x[2] + x[3] * x[3]
            kinetic = x[2] * lap[2] + x[3] * lap[3]
            sums[0, z, 0] = jnp.where(top, dense, pltpu.roll(kinetic, 4, 0))
            sums[1, z, 0] = jnp.where(top, pltpu.roll(dense, 4, 0), kinetic)

    def copy_to(src, dst, send_sem, recv_sem, peer):
        copy = pltpu.make_async_remote_copy(
            src_ref=src,
            dst_ref=dst,
            send_sem=send_sem,
            recv_sem=recv_sem,
            device_id=peer,
            device_id_type=MESH,
        )
        copy.start()
        return copy

    order = sorted(range(1, n), key=lambda d: -min(d, n - d))
    first_copies = []
    for d in order + [0]:
        planes = pl.ds(second_at[d] * share, share)
        first_copies.append(
            copy_to(sums.at[1 - core, planes], piece_in.at[n + d], first_send.at[n + d], first_recv.at[n + d], second_cross[d])
        )
        if d > 0:
            planes = pl.ds(first_at[d] * share, share)
            first_copies.append(
                copy_to(sums.at[core, planes], piece_in.at[d], first_send.at[d], first_recv.at[d], first_peer[d])
            )
    total = sums[core, pl.ds(first * share, share)]
    for copy in first_copies:
        copy.wait_recv()
    for d in range(1, 2 * n):
        total = total + piece_in[d]
    gather_in[0] = total

    second_copies = [
        copy_to(gather_in.at[0], gather_in.at[d], second_send.at[d - 1], second_recv.at[d - 1], second_peer[d])
        for d in order
    ]
    for copy in second_copies:
        copy.wait_recv()
    total = gather_in[second]
    for i in range(1, n):
        total = total + gather_in[lax.rem(second + n - i, n)]

    for z in range(share):
        s01, s23 = total[z, 0], total[z, 1]
        density = (2.0 / modes_total) * s01
        kinetic = (-2.0 / modes_total) * pltpu.roll(s01, 4, 0)
        an_re = (1.0 / modes_total) * s23
        an_im = (1.0 / modes_total) * pltpu.roll(s23, 4, 0)
        dense = jnp.where(top, density, jnp.float32(1.0)) + EPS
        third_root = jnp.exp(jnp.log(dense) * (-1.0 / 3.0))
        fermi = (0.5 * (3.0 * math.pi**2) ** (2.0 / 3.0)) * (dense * third_root)
        an_sq = an_re * an_re + an_im * an_im
        f0 = BETA * fermi - (GAMMA / 3.0) * an_sq * third_root / dense
        f1 = -GAMMA * an_re * third_root
        f2 = -GAMMA * an_im * third_root
        f3 = (0.5 * ALPHA) * kinetic + (0.6 * BETA) * dense * fermi + GAMMA * an_sq * third_root
        field_mine[0, z, 0] = jnp.where(top, f0, pltpu.roll(f1, 4, 0))
        field_mine[0, z, 1] = jnp.where(top, f2, pltpu.roll(f3, 4, 0))

    back_copies = []
    for d in order + [0]:
        back_copies.append(
            copy_to(field_mine.at[0], field_other.at[d], back_send.at[n + d], back_recv.at[n + d], first_cross[d])
        )
        if d > 0:
            back_copies.append(copy_to(field_mine.at[0], field_mine.at[d], back_send.at[d], back_recv.at[d], first_peer[d]))
    for copy in back_copies:
        copy.wait_recv()

    even = core == 0
    for z in range(PLANES):
        place, part = z // share, z % share
        mine = field_mine[lax.rem(first + n - place, n), part]
        other = field_other[lax.rem(second + n - place, n), part]
        fields = []
        for p in range(2):
            low = jnp.where(even, mine[p], other[p])
            high = jnp.where(even, other[p], mine[p])
            fields.append(jnp.where(top, low, pltpu.roll(high, 4, 0)))
            fields.append(jnp.where(top, pltpu.roll(low, 4, 0), high))
        for c in range(3):
            pots[z, c] = fields[c]
        for c in range(4):
            field_rows[c, z * ROWS : (z + 1) * ROWS, :] = fields[c]
        x = xs[4, z]
        k = slope(x, base[z], fields[0], fields[1], fields[2])
        for c in range(4):
            acc[z, c] = x[c] + (DT / 6.0) * k[c]
            xs[5, z, c] = x[c] + (0.5 * DT) * k[c]
        if z == 3:
            send(5, 0)
    send(5, 1)
    own_plane(5)
    for z in range(PLANES):
        k = slope(xs[5, z], own_part(5, z), pots[z, 0], pots[z, 1], pots[z, 2])
        for c in range(4):
            acc[z, c] = acc[z, c] + (DT / 3.0) * k[c]
    for side in (0, 1):
        for z in arrived(5, side):
            more = turned(halo_part(5, z, -0.5 * ALPHA * DT / 3.0))
            for c in range(4):
                out_rows[c, z * ROWS : (z + 1) * ROWS, :] = acc[z, c] + more[c]

    for s in range(6):
        to_left(s).wait_send()
        to_right(s).wait_send()
    for copy in first_copies + second_copies + back_copies:
        copy.wait_send()


def unpack(out_rows, field_rows, uo_ref, vo_ref, fo_ref, outs, sems):
    copies = [
        pltpu.make_async_copy(outs.at[0:4], fo_ref, sems.at[0]),
        pltpu.make_async_copy(outs.at[4:6], uo_ref.at[0], sems.at[1]),
        pltpu.make_async_copy(outs.at[6:8], vo_ref.at[0], sems.at[2]),
    ]
    for c in range(8):
        source = field_rows if c < 4 else out_rows
        for t in range(ROWS):
            outs[c, :, t * LANES : (t + 1) * LANES] = source[c % 4, pl.ds(t, PLANES, stride=ROWS), :]
        if c in (3, 5, 7):
            copies[(c - 3) // 2].start()
    for copy in copies:
        copy.wait()


def solution(mesh):
    modes, grid_n = mesh.shape["modes"], mesh.shape["grid"]
    n = math.isqrt(modes // 2)
    share = PLANES // n
    f32 = jnp.float32
    plane = (ROWS, LANES)
    vmem = pl.BlockSpec(memory_space=pltpu.VMEM)
    hbm = pl.BlockSpec(memory_space=pltpu.HBM)

    def local(u_modes, v_modes, potential, pairing):
        out_rows, field_rows = pl.pallas_call(
            functools.partial(kernel, n, grid_n, float(modes)),
            out_shape=(jax.ShapeDtypeStruct((4, PLANES * ROWS, LANES), f32),) * 2,
            in_specs=[hbm] * 4,
            out_specs=(vmem, vmem),
            scratch_shapes=[
                pltpu.VMEM((7, PLANES, ROWS * LANES), f32),
                pltpu.VMEM((7, PLANES * ROWS, LANES), f32),
                pltpu.VMEM((6, PLANES, 4) + plane, f32),
                pltpu.VMEM((PLANES, 3) + plane, f32),
                pltpu.VMEM((PLANES, 4) + plane, f32),
                pltpu.VMEM((PLANES, 4) + plane, f32),
                pltpu.VMEM((PLANES, 4) + plane, f32),
                pltpu.VMEM((6, 4, 4) + plane, f32),
                pltpu.VMEM((6, 4, 4) + plane, f32),
                pltpu.VMEM((2, PLANES, 2) + plane, f32),
                pltpu.VMEM((2 * n, share, 2) + plane, f32),
                pltpu.VMEM((n, share, 2) + plane, f32),
                pltpu.VMEM((n, share, 2) + plane, f32),
                pltpu.VMEM((n, share, 2) + plane, f32),
                pltpu.VMEM((3, 2 * LANES, 2 * LANES), jnp.bfloat16),
                pltpu.SemaphoreType.DMA((4,)),
                pltpu.SemaphoreType.DMA((2, 6)),
                pltpu.SemaphoreType.DMA((2, 6)),
                pltpu.SemaphoreType.DMA((2 * n,)),
                pltpu.SemaphoreType.DMA((2 * n,)),
                pltpu.SemaphoreType.DMA((n - 1,)),
                pltpu.SemaphoreType.DMA((n - 1,)),
                pltpu.SemaphoreType.DMA((2 * n,)),
                pltpu.SemaphoreType.DMA((2 * n,)),
            ],
            compiler_params=pltpu.CompilerParams(
                collective_id=0, has_side_effects=True, vmem_limit_bytes=16 * 1024 * 1024
            ),
        )(*(pltpu.with_memory_space_constraint(x, pltpu.HBM) for x in (u_modes, v_modes, potential, pairing)))
        return pl.pallas_call(
            unpack,
            out_shape=(
                jax.ShapeDtypeStruct(u_modes.shape, f32),
                jax.ShapeDtypeStruct(v_modes.shape, f32),
                jax.ShapeDtypeStruct((4,) + potential.shape, f32),
            ),
            in_specs=[vmem, vmem],
            out_specs=(hbm, hbm, hbm),
            scratch_shapes=[
                pltpu.VMEM((8, PLANES, ROWS * LANES), f32),
                pltpu.SemaphoreType.DMA((3,)),
            ],
            compiler_params=pltpu.CompilerParams(vmem_limit_bytes=16 * 1024 * 1024),
        )(out_rows, field_rows)

    placed = (
        P("modes", None, "grid", None),
        P("modes", None, "grid", None),
        P("grid", None),
        P(None, "grid", None),
    )
    return jax.shard_map(
        local,
        mesh=mesh,
        in_specs=placed,
        out_specs=(placed[0], placed[1], placed[3]),
        check_vma=False,
    )
```

time: 67.7 us -> 61.8 us (0.913)
  local copies, waits for them, and re-layouts: 5.18 us -> 0 us
  Pallas kernels: 61.6 us -> 60.9 us
    unnamed x11 -> x0, local copies, waits for them, and re-layouts: 5.18 us -> none
    pallas_call x1, Pallas kernels: 61.6 us -> 60.2 us  [local(): pl.pallas_call(functools.partial(kernel, n, grid_n, float(modes)), out_sh...]
    pallas_call x0 -> x1, Pallas kernels: none -> 0.75 us  [local(): pl.pallas_call(unpack, out_shape=(jax.ShapeDtypeStruct(u_modes.shape, f32...]
where the time goes in v2:
time: 61.8 us; the launch traced here: 61.6 us
  Pallas kernels  60.9 us (99%)
  between operations  0.64 us (1%)
    pallas_call x1, Pallas kernels, local(): pl.pallas_call(functools.partial(kernel, n, grid_n, float(modes)), out_sh...  60.2 us

profile of v2, /device:TPU:1, one launch (start us, length us, event | category | flops | bytes accessed | tf_op | source)
XLA Modules:
  0.0 61.6 jit_solution(13084747467447835859)
XLA Ops:
  0.6 60.2 %shard_map.67 = (f32[4,64,128]{2,1,0:T(8,128)S(1)}, f32[4,64,128]{2,1,0:T(8,128)S(1)}) custom-call(f32[1,2,8,1024]{3,2,1,0:T(8,128)} %u_ref.1, f32[1,2,8,1024]{3,2,1,0:T(8,128)} %v_ref.1, f32[8,1024]{1,0:T(8,128)} %pot_ref.1, f32[2,8,1024]{2,1,0:T(8,128)} %pair_ref.1), custom_call_target="tpu_custom_call" | custom-call | tf_op jit(solution)/shard_map/pallas_call | solution.py:388
  60.8 0.7 %shard_map.68 = (f32[1,2,8,1024]{3,2,1,0:T(8,128)}, f32[1,2,8,1024]{3,2,1,0:T(8,128)}, f32[4,8,1024]{2,1,0:T(8,128)}) custom-call(f32[4,64,128]{2,1,0:T(8,128)S(1)} %get-tuple-element.5.out_rows, f32[4,64,128]{2,1,0:T(8,128)S(1)} %get-tuple-element.6.field_rows), custom_call_target="tpu_custom_call" | custom-call | tf_op jit(solution)/shard_map/pallas_call | solution.py:423

commit v3 on v2

v3 whole, which is shorter than its diff:
```python
import functools
import math

import jax
import jax.numpy as jnp
from jax import lax
from jax.experimental import pallas as pl
from jax.experimental.pallas import tpu as pltpu
from jax.sharding import PartitionSpec as P

MESH = pl.DeviceIdType.MESH
COEF = (-205.0 / 72.0, 8.0 / 5.0, -1.0 / 5.0, 8.0 / 315.0, -1.0 / 560.0)
ALPHA = 1.14
BETA = -0.553
GAMMA = -11.11
DT = 0.18
EPS = 1e-06
PLANES = 8
ROWS = 8
LANES = 128


def spread(weights):
    source = lax.broadcasted_iota(jnp.int32, (LANES, LANES), 0)
    target = lax.broadcasted_iota(jnp.int32, (LANES, LANES), 1)
    dx = lax.rem(lax.rem(source, 32) + 32 - lax.rem(target, 32), 32)
    dy = source // 32 - target // 32
    zero = jnp.zeros((LANES, LANES), jnp.float32)
    within, above, below = zero, zero, zero
    for k in range(1, 5):
        within = jnp.where((dy == 0) & ((dx == k) | (dx == 32 - k)), COEF[k], within)
        within = jnp.where((dx == 0) & ((dy == k) | (dy == -k)), COEF[k], within)
        above = jnp.where((dx == 0) & (dy + 4 == k), COEF[k], above)
        below = jnp.where((dx == 0) & (4 - dy == k), COEF[k], below)
    for i, part in enumerate((within, above, below)):
        high = part.astype(jnp.bfloat16)
        low = (part - high.astype(jnp.float32)).astype(jnp.bfloat16)
        for half in range(2):
            weights[i, LANES * half : LANES * (half + 1), 0:LANES] = high
            weights[i, LANES * half : LANES * (half + 1), LANES : 2 * LANES] = low


def in_plane(x, weights):
    flat = x.reshape(-1, LANES)
    high = flat.astype(jnp.bfloat16)
    low = (flat - high.astype(jnp.float32)).astype(jnp.bfloat16)
    both = jnp.concatenate([high, low], axis=1)

    def times(i):
        wide = jnp.dot(both, weights[i], preferred_element_type=jnp.float32)
        return (wide[:, :LANES] + wide[:, LANES:]).reshape(x.shape)

    return (3.0 * COEF[0]) * x + times(0) + pltpu.roll(times(1), ROWS - 1, 1) + pltpu.roll(times(2), 1, 1)


def slope(x, lap, pot, pr, pi):
    kin = [(-0.5 * ALPHA) * lap[c] + pot * x[c] for c in range(4)]
    return [
        kin[1] + pr * x[3] + pi * x[2],
        pi * x[3] - pr * x[2] - kin[0],
        pr * x[1] - pi * x[0] - kin[3],
        kin[2] - pr * x[0] - pi * x[1],
    ]


def kernel(
    n,
    grid_n,
    modes_total,
    u_ref,
    v_ref,
    pot_ref,
    pair_ref,
    out_rows,
    field_rows,
    raws,
    rows,
    wide,
    inner,
    middle,
    pots,
    acc,
    base,
    own,
    sums,
    taus,
    piece_in,
    gather_in,
    field_mine,
    field_other,
    tau_piece,
    tau_gather,
    energy_mine,
    energy_other,
    weights,
    load_sem,
    ring_send,
    ring_recv,
    first_send,
    first_recv,
    second_send,
    second_recv,
    back_send,
    back_recv,
):
    m = lax.axis_index("modes")
    g = lax.axis_index("grid")
    core = lax.rem(m, 2)
    yy = lax.rem(m // 2, n)
    zz = m // (2 * n)
    left = (m, lax.rem(g + grid_n - 1, grid_n))
    right = (m, lax.rem(g + 1, grid_n))
    flip = 1 - 2 * core
    first = yy + core * (zz - yy)
    second = zz + core * (yy - zz)
    first_base = (1 - core) * zz * 2 * n + core * (yy * 2 + 1)
    first_step = 2 + core * (2 * n - 2)
    second_base = (1 - core) * yy * 2 + core * (zz * 2 * n + 1)
    second_step = 2 * n - core * (2 * n - 2)
    share = PLANES // n
    first_at = [lax.rem(first + d, n) for d in range(n)]
    second_at = [lax.rem(second + d, n) for d in range(n)]
    first_peer = [(first_base + at * first_step, g) for at in first_at]
    second_peer = [(second_base + at * second_step, g) for at in second_at]
    first_cross = [(peer[0] + flip, g) for peer in first_peer]
    second_cross = [(peer[0] + flip, g) for peer in second_peer]
    order = sorted(range(1, n), key=lambda d: -min(d, n - d))
    started = []

    def remote(src, dst, send_sem, recv_sem, peer):
        copy = pltpu.make_async_remote_copy(
            src_ref=src,
            dst_ref=dst,
            send_sem=send_sem,
            recv_sem=recv_sem,
            device_id=peer,
            device_id_type=MESH,
        )
        started.append(copy)
        return copy

    def to_left(k, src, dst):
        return remote(src, dst, ring_send.at[0, k], ring_recv.at[0, k], left)

    def to_right(k, src, dst):
        return remote(src, dst, ring_send.at[1, k], ring_recv.at[1, k], right)

    barrier = pltpu.get_barrier_semaphore()
    partners = [left, right] + first_cross + first_peer[1:] + second_peer[1:] + second_cross[1:]
    for partner in partners:
        pl.semaphore_signal(barrier, inc=1, device_id=partner, device_id_type=MESH)

    loads = [
        pltpu.make_async_copy(u_ref.at[0], raws.at[1, 0:2], load_sem.at[0]),
        pltpu.make_async_copy(v_ref.at[0], raws.at[1, 2:4], load_sem.at[1]),
        pltpu.make_async_copy(pot_ref, raws.at[1, 4], load_sem.at[2]),
        pltpu.make_async_copy(pair_ref, raws.at[1, 5:7], load_sem.at[3]),
    ]
    for load in loads:
        load.start()
    low, high = slice(0, 4), slice(4, 8)
    start_copies = [[], []]
    for k, planes in ((0, (low, high)), (2, (high, low))):
        for side, send in enumerate((to_left, to_right)):
            place = 2 - 2 * side
            at = planes[side]
            start_copies[side] += [
                send(k, u_ref.at[0, :, at, :], raws.at[place, 0:2, at, :]),
                send(k + 1, v_ref.at[0, :, at, :], raws.at[place, 2:4, at, :]),
            ]
    for side, send in enumerate((to_left, to_right)):
        place = 2 - 2 * side
        at = (low, high)[side]
        start_copies[side] += [
            send(4, pot_ref.at[at, :], raws.at[place, 4, at, :]),
            send(5, pair_ref.at[:, at, :], raws.at[place, 5:7, at, :]),
        ]
    pl.semaphore_wait(barrier, len(partners))
    for i in (0, 1, 4, 5, 2, 3):
        for side in (0, 1):
            start_copies[side][i].start()

    spread(weights)
    row = lax.broadcasted_iota(jnp.int32, (ROWS, LANES), 0)
    top = row < 4

    def planes_of(place, comps, at):
        for c in comps:
            for t in range(ROWS):
                piece = raws[place, c, at, t * LANES : (t + 1) * LANES]
                rows[c, t * PLANES + at.start : t * PLANES + at.stop, :] = piece
        for c in comps:
            for z in range(at.start, at.stop):
                yield c, z, rows[c, pl.ds(z, ROWS, stride=PLANES), :]

    def flat_plane(x):
        return in_plane(x.reshape(-1, ROWS, LANES), weights).reshape(x.shape)

    def depth(ref, z):
        total = COEF[1] * (ref[z - 1] + ref[z + 1])
        for k in range(2, 5):
            total = total + COEF[k] * (ref[z - k] + ref[z + k])
        return total

    for load in loads:
        load.wait()
    for c, z, value in planes_of(1, range(7), slice(0, 8)):
        if c < 4:
            wide[0, 8 + z, c] = value
        else:
            pots[4 + z, c - 4] = value

    def section(s, arrive, reach, weight):
        def advance(z):
            lap = base[z - 4] + depth(wide.at[s], z)
            k = slope(wide[s, z], lap, pots[z - 4, 0], pots[z - 4, 1], pots[z - 4, 2])
            for c in range(4):
                inner[z - 4, c] = wide[0, z, c] + reach * k[c]
                if 8 <= z < 16:
                    acc[z - 8, c] = (wide[0, z, c] if s == 0 else acc[z - 8, c]) + weight * k[c]

        base[4:12] = flat_plane(wide[s, 8:16])
        for side in (0, 1):
            arrive(side, 0)
            for z in range(8 + 4 * side, 12 + 4 * side):
                advance(z)
        own[...] = flat_plane(inner[4:12])
        base[0:4] = flat_plane(wide[s, 4:8])
        base[12:16] = flat_plane(wide[s, 16:20])
        for side in (0, 1):
            arrive(side, 1)
            for z in range(4 + 12 * side, 8 + 12 * side):
                advance(z)

    def second_slope(z):
        lap = own[z] + depth(inner, z + 4)
        return slope(inner[z + 4], lap, pots[z + 4, 0], pots[z + 4, 1], pots[z + 4, 2])

    def arrive_start(side, far):
        copies = start_copies[1 - side]
        place, at = ((0, (high, low)), (2, (low, high)))[side]
        for copy in copies[2:4] if far else copies[0:2]:
            copy.wait_recv()
        for c, z, value in planes_of(place, range(4), at[far]):
            wide[0, 8 * place + z, c] = value
        if far:
            for copy in copies[4:6]:
                copy.wait_recv()
            for c, z, value in planes_of(place, range(4, 7), at[0]):
                pots[8 * place - 4 + z, c - 4] = value

    section(0, arrive_start, 0.5 * DT, DT / 6.0)
    near = [to_left(6, wide.at[1, 8:12], wide.at[1, 16:20]), to_right(6, wide.at[1, 12:16], wide.at[1, 4:8])]
    far = [to_left(7, wide.at[1, 12:16], wide.at[1, 20:24]), to_right(7, wide.at[1, 8:12], wide.at[1, 0:4])]
    for z in range(PLANES):
        k = second_slope(z)
        for c in range(4):
            wide[1, 8 + z, c] = wide[0, 8 + z, c] + (0.5 * DT) * k[c]
            acc[z, c] = acc[z, c] + (DT / 3.0) * k[c]
        if z == 3:
            near[0].start()
    near[1].start()
    far[0].start()
    far[1].start()

    def arrive_second(side, is_far):
        (far if is_far else near)[1 - side].wait_recv()

    section(1, arrive_second, DT, DT / 3.0)
    edge = [to_left(8, wide.at[2, 8:12], wide.at[2, 16:20]), to_right(8, wide.at[2, 12:16], wide.at[2, 4:8])]
    for z in range(PLANES):
        k = second_slope(z)
        x = [acc[z, c] + (DT / 6.0) * k[c] for c in range(4)]
        for c in range(4):
            wide[2, 8 + z, c] = x[c]
        dense = x[2] * x[2] + x[3] * x[3]
        an_re = x[0] * x[2] + x[1] * x[3]
        an_im = x[1] * x[2] - x[0] * x[3]
        sums[0, z, 0] = jnp.where(top, dense, pltpu.roll(an_re, 4, 0))
        sums[1, z, 0] = jnp.where(top, pltpu.roll(dense, 4, 0), an_re)
        sums[0, z, 1] = an_im
        sums[1, z, 1] = pltpu.roll(an_im, 4, 0)

    def to_owners(lot, src, piece):
        copies = []
        for d in order + [0]:
            planes = pl.ds(second_at[d] * share, share)
            at = (lot, n + d)
            copies.append(
                remote(src.at[1 - core, planes], piece.at[n + d], first_send.at[at], first_recv.at[at], second_cross[d])
            )
            if d > 0:
                planes = pl.ds(first_at[d] * share, share)
                copies.append(
                    remote(src.at[core, planes], piece.at[d], first_send.at[lot, d], first_recv.at[lot, d], first_peer[d])
                )
        for copy in copies:
            copy.start()
        return copies

    def summed(copies, src, piece):
        total = src[core, pl.ds(first * share, share)]
        for copy in copies:
            copy.wait_recv()
        for d in range(1, 2 * n):
            total = total + piece[d]
        return total

    def along_second(lot, gather, value):
        gather[0] = value
        copies = []
        for d in order:
            copy = remote(gather.at[0], gather.at[d], second_send.at[lot, d], second_recv.at[lot, d], second_peer[d])
            copy.start()
            copies.append(copy)
        return copies

    def gathered(copies, gather):
        for copy in copies:
            copy.wait_recv()
        total = gather[second]
        for i in range(1, n):
            total = total + gather[lax.rem(second + n - i, n)]
        return total

    def back(lot, mine, other):
        copies = []
        for d in order + [0]:
            at = (lot, n + d)
            copies.append(remote(mine.at[0], other.at[d], back_send.at[at], back_recv.at[at], first_cross[d]))
            if d > 0:
                copies.append(remote(mine.at[0], mine.at[d], back_send.at[lot, d], back_recv.at[lot, d], first_peer[d]))
        for copy in copies:
            copy.start()
        return copies

    main_first = to_owners(0, sums, piece_in)
    edge[0].start()
    edge[1].start()

    own[...] = flat_plane(wide[2, 8:16])
    for side in (0, 1):
        edge[1 - side].wait_recv()
        for z in range(4 * side, 4 * side + 4):
            lap = own[z]
            for k in range(1, 5):
                lap = lap + COEF[k] * (wide[2, 8 + z - k] + wide[2, 8 + z + k])
            own[z] = lap
            kinetic = wide[2, 8 + z, 2] * lap[2] + wide[2, 8 + z, 3] * lap[3]
            taus[0, z] = kinetic
            taus[1, z] = pltpu.roll(kinetic, 4, 0)
    tau_first = to_owners(1, taus, tau_piece)
    main_second = along_second(0, gather_in, summed(main_first, sums, piece_in))
    tau_second = along_second(1, tau_gather, summed(tau_first, taus, tau_piece))
    total = gathered(main_second, gather_in)

    rests = []
    for z in range(share):
        dense = jnp.where(top, (2.0 / modes_total) * total[z, 0], jnp.float32(1.0)) + EPS
        an_re = (1.0 / modes_total) * pltpu.roll(total[z, 0], 4, 0)
        an_im = (1.0 / modes_total) * total[z, 1]
        third_root = jnp.exp(jnp.log(dense) * (-1.0 / 3.0))
        fermi = (0.5 * (3.0 * math.pi**2) ** (2.0 / 3.0)) * (dense * third_root)
        an_sq = an_re * an_re + an_im * an_im
        f0 = BETA * fermi - (GAMMA / 3.0) * an_sq * third_root / dense
        f1 = -GAMMA * an_re * third_root
        f2 = -GAMMA * an_im * third_root
        rests.append((0.6 * BETA) * dense * fermi + GAMMA * an_sq * third_root)
        field_mine[0, z, 0] = jnp.where(top, f0, pltpu.roll(f1, 4, 0))
        field_mine[0, z, 1] = f2
    main_back = back(0, field_mine, field_other)
    tau_total = gathered(tau_second, tau_gather)
    for z in range(share):
        energy_mine[0, z] = (-ALPHA / modes_total) * tau_total[z] + rests[z]
    tau_back = back(1, energy_mine, energy_other)
    for copy in main_back:
        copy.wait_recv()

    even = core == 0
    swap = [to_left(9, middle.at[4:8], middle.at[12:16]), to_right(9, middle.at[8:12], middle.at[0:4])]

    def places(z):
        place = z // share
        return lax.rem(first + n - place, n), lax.rem(second + n - place, n), z % share

    for z in range(PLANES):
        at_mine, at_other, part = places(z)
        mine, other = field_mine[at_mine, part], field_other[at_other, part]
        lower = [jnp.where(even, mine[p], other[p]) for p in range(2)]
        upper = [jnp.where(even, other[p], mine[p]) for p in range(2)]
        fields = [
            jnp.where(top, lower[0], pltpu.roll(upper[0], 4, 0)),
            jnp.where(top, pltpu.roll(lower[0], 4, 0), upper[0]),
            jnp.where(top, lower[1], pltpu.roll(upper[1], 4, 0)),
        ]
        k = slope(wide[2, 8 + z], own[z], *fields)
        for c in range(3):
            pots[z + 4, c] = fields[c]
            field_rows[c, z * ROWS : (z + 1) * ROWS, :] = fields[c]
        for c in range(4):
            acc[z, c] = wide[2, 8 + z, c] + (DT / 6.0) * k[c]
            middle[4 + z, c] = wide[2, 8 + z, c] + (0.5 * DT) * k[c]
        if z == 3:
            swap[0].start()
    swap[1].start()
    own[...] = flat_plane(middle[4:12])
    for copy in tau_back:
        copy.wait_recv()
    for z in range(PLANES):
        at_mine, at_other, part = places(z)
        mine, other = energy_mine[at_mine, part], energy_other[at_other, part]
        lower, upper = jnp.where(even, mine, other), jnp.where(even, other, mine)
        field_rows[3, z * ROWS : (z + 1) * ROWS, :] = jnp.where(top, lower, pltpu.roll(upper, 4, 0))
    for side in (0, 1):
        swap[1 - side].wait_recv()
        for z in range(4 * side, 4 * side + 4):
            lap = own[z] + depth(middle, z + 4)
            k = slope(middle[4 + z], lap, pots[z + 4, 0], pots[z + 4, 1], pots[z + 4, 2])
            for c in range(4):
                out_rows[c, z * ROWS : (z + 1) * ROWS, :] = acc[z, c] + (DT / 3.0) * k[c]

    for copy in started:
        copy.wait_send()


def unpack(out_rows, field_rows, uo_ref, vo_ref, fo_ref, outs, sems):
    copies = [
        pltpu.make_async_copy(outs.at[0:4], fo_ref, sems.at[0]),
        pltpu.make_async_copy(outs.at[4:6], uo_ref.at[0], sems.at[1]),
        pltpu.make_async_copy(outs.at[6:8], vo_ref.at[0], sems.at[2]),
    ]
    for c in range(8):
        source = field_rows if c < 4 else out_rows
        for t in range(ROWS):
            outs[c, :, t * LANES : (t + 1) * LANES] = source[c % 4, pl.ds(t, PLANES, stride=ROWS), :]
        if c in (3, 5, 7):
            copies[(c - 3) // 2].start()
    for copy in copies:
        copy.wait()


def solution(mesh):
    modes, grid_n = mesh.shape["modes"], mesh.shape["grid"]
    n = math.isqrt(modes // 2)
    share = PLANES // n
    f32 = jnp.float32
    plane = (ROWS, LANES)
    vmem = pl.BlockSpec(memory_space=pltpu.VMEM)
    hbm = pl.BlockSpec(memory_space=pltpu.HBM)

    def local(u_modes, v_modes, potential, pairing):
        out_rows, field_rows = pl.pallas_call(
            functools.partial(kernel, n, grid_n, float(modes)),
            out_shape=(jax.ShapeDtypeStruct((4, PLANES * ROWS, LANES), f32),) * 2,
            in_specs=[hbm] * 4,
            out_specs=(vmem, vmem),
            scratch_shapes=[
                pltpu.VMEM((3, 7, PLANES, ROWS * LANES), f32),
                pltpu.VMEM((7, PLANES * ROWS, LANES), f32),
                pltpu.VMEM((3, 3 * PLANES, 4) + plane, f32),
                pltpu.VMEM((2 * PLANES, 4) + plane, f32),
                pltpu.VMEM((2 * PLANES, 4) + plane, f32),
                pltpu.VMEM((2 * PLANES, 3) + plane, f32),
                pltpu.VMEM((PLANES, 4) + plane, f32),
                pltpu.VMEM((2 * PLANES, 4) + plane, f32),
                pltpu.VMEM((PLANES, 4) + plane, f32),
                pltpu.VMEM((2, PLANES, 2) + plane, f32),
                pltpu.VMEM((2, PLANES) + plane, f32),
                pltpu.VMEM((2 * n, share, 2) + plane, f32),
                pltpu.VMEM((n, share, 2) + plane, f32),
                pltpu.VMEM((n, share, 2) + plane, f32),
                pltpu.VMEM((n, share, 2) + plane, f32),
                pltpu.VMEM((2 * n, share) + plane, f32),
                pltpu.VMEM((n, share) + plane, f32),
                pltpu.VMEM((n, share) + plane, f32),
                pltpu.VMEM((n, share) + plane, f32),
                pltpu.VMEM((3, 2 * LANES, 2 * LANES), jnp.bfloat16),
                pltpu.SemaphoreType.DMA((4,)),
                pltpu.SemaphoreType.DMA((2, 10)),
                pltpu.SemaphoreType.DMA((2, 10)),
                pltpu.SemaphoreType.DMA((2, 2 * n)),
                pltpu.SemaphoreType.DMA((2, 2 * n)),
                pltpu.SemaphoreType.DMA((2, n)),
                pltpu.SemaphoreType.DMA((2, n)),
                pltpu.SemaphoreType.DMA((2, 2 * n)),
                pltpu.SemaphoreType.DMA((2, 2 * n)),
            ],
            compiler_params=pltpu.CompilerParams(
                collective_id=0, has_side_effects=True, vmem_limit_bytes=16 * 1024 * 1024
            ),
        )(*(pltpu.with_memory_space_constraint(x, pltpu.HBM) for x in (u_modes, v_modes, potential, pairing)))
        return pl.pallas_call(
            unpack,
            out_shape=(
                jax.ShapeDtypeStruct(u_modes.shape, f32),
                jax.ShapeDtypeStruct(v_modes.shape, f32),
                jax.ShapeDtypeStruct((4,) + potential.shape, f32),
            ),
            in_specs=[vmem, vmem],
            out_specs=(hbm, hbm, hbm),
            scratch_shapes=[
                pltpu.VMEM((8, PLANES, ROWS * LANES), f32),
                pltpu.SemaphoreType.DMA((3,)),
            ],
            compiler_params=pltpu.CompilerParams(vmem_limit_bytes=16 * 1024 * 1024),
        )(out_rows, field_rows)

    placed = (
        P("modes", None, "grid", None),
        P("modes", None, "grid", None),
        P("grid", None),
        P(None, "grid", None),
    )
    return jax.shard_map(
        local,
        mesh=mesh,
        in_specs=placed,
        out_specs=(placed[0], placed[1], placed[3]),
        check_vma=False,
    )
```

time: 61.8 us -> 55.7 us (0.901)
  Pallas kernels: 60.9 us -> 55 us
    pallas_call x1, Pallas kernels: 60.2 us -> 54.2 us  [local(): pl.pallas_call(functools.partial(kernel, n, grid_n, float(modes)), out_sh...]
where the time goes in v3:
time: 55.7 us; the launch traced here: 55.6 us
  Pallas kernels  55 us (99%)
  between operations  0.64 us (1%)
    pallas_call x1, Pallas kernels, local(): pl.pallas_call(functools.partial(kernel, n, grid_n, float(modes)), out_sh...  54.2 us

profile of v3, /device:TPU:1, one launch (start us, length us, event | category | flops | bytes accessed | tf_op | source)
XLA Modules:
  0.0 55.6 jit_solution(10624395771918968678)
XLA Ops:
  0.6 54.2 %shard_map.67 = (f32[4,64,128]{2,1,0:T(8,128)S(1)}, f32[4,64,128]{2,1,0:T(8,128)S(1)}) custom-call(f32[1,2,8,1024]{3,2,1,0:T(8,128)} %u_ref.1, f32[1,2,8,1024]{3,2,1,0:T(8,128)} %v_ref.1, f32[8,1024]{1,0:T(8,128)} %pot_ref.1, f32[2,8,1024]{2,1,0:T(8,128)} %pair_ref.1), custom_call_target="tpu_custom_call" | custom-call | tf_op jit(solution)/shard_map/pallas_call | solution.py:452
  54.8 0.7 %shard_map.68 = (f32[1,2,8,1024]{3,2,1,0:T(8,128)}, f32[1,2,8,1024]{3,2,1,0:T(8,128)}, f32[4,8,1024]{2,1,0:T(8,128)}) custom-call(f32[4,64,128]{2,1,0:T(8,128)S(1)} %get-tuple-element.5.out_rows, f32[4,64,128]{2,1,0:T(8,128)S(1)} %get-tuple-element.6.field_rows), custom_call_target="tpu_custom_call" | custom-call | tf_op jit(solution)/shard_map/pallas_call | solution.py:492

commit v4 on v3

v4 whole, which is shorter than its diff:
```python
import functools
import math

import jax
import jax.numpy as jnp
from jax import lax
from jax.experimental import pallas as pl
from jax.experimental.pallas import tpu as pltpu
from jax.sharding import PartitionSpec as P

MESH = pl.DeviceIdType.MESH
COEF = (-205.0 / 72.0, 8.0 / 5.0, -1.0 / 5.0, 8.0 / 315.0, -1.0 / 560.0)
ALPHA = 1.14
BETA = -0.553
GAMMA = -11.11
DT = 0.18
EPS = 1e-06
PLANES = 8
ROWS = 8
LANES = 128


def spread(weights):
    source = lax.broadcasted_iota(jnp.int32, (LANES, LANES), 0)
    target = lax.broadcasted_iota(jnp.int32, (LANES, LANES), 1)
    dx = lax.rem(lax.rem(source, 32) + 32 - lax.rem(target, 32), 32)
    dy = source // 32 - target // 32
    zero = jnp.zeros((LANES, LANES), jnp.float32)
    within, above, below = zero, zero, zero
    for k in range(1, 5):
        within = jnp.where((dy == 0) & ((dx == k) | (dx == 32 - k)), COEF[k], within)
        within = jnp.where((dx == 0) & ((dy == k) | (dy == -k)), COEF[k], within)
        above = jnp.where((dx == 0) & (dy + 4 == k), COEF[k], above)
        below = jnp.where((dx == 0) & (4 - dy == k), COEF[k], below)
    for i, part in enumerate((within, above, below)):
        high = part.astype(jnp.bfloat16)
        low = (part - high.astype(jnp.float32)).astype(jnp.bfloat16)
        for half in range(2):
            weights[i, LANES * half : LANES * (half + 1), 0:LANES] = high
            weights[i, LANES * half : LANES * (half + 1), LANES : 2 * LANES] = low


def in_plane(x, weights):
    flat = x.reshape(-1, LANES)
    high = flat.astype(jnp.bfloat16)
    low = (flat - high.astype(jnp.float32)).astype(jnp.bfloat16)
    both = jnp.concatenate([high, low], axis=1)

    def times(i):
        wide = jnp.dot(both, weights[i], preferred_element_type=jnp.float32)
        return (wide[:, :LANES] + wide[:, LANES:]).reshape(x.shape)

    return (3.0 * COEF[0]) * x + times(0) + pltpu.roll(times(1), ROWS - 1, 1) + pltpu.roll(times(2), 1, 1)


def slope(x, lap, pot, pr, pi):
    kin = [(-0.5 * ALPHA) * lap[c] + pot * x[c] for c in range(4)]
    return [
        kin[1] + pr * x[3] + pi * x[2],
        pi * x[3] - pr * x[2] - kin[0],
        pr * x[1] - pi * x[0] - kin[3],
        kin[2] - pr * x[0] - pi * x[1],
    ]


def kernel(
    n,
    grid_n,
    modes_total,
    u_ref,
    v_ref,
    pot_ref,
    pair_ref,
    out_rows,
    field_rows,
    raw,
    rows,
    wide,
    inner,
    middle,
    pots,
    acc,
    base,
    own,
    sums,
    taus,
    piece_in,
    gather_in,
    field_mine,
    field_other,
    tau_piece,
    tau_gather,
    energy_mine,
    energy_other,
    weights,
    load_sem,
    ring_send,
    ring_recv,
    y_send,
    y_recv,
    z_send,
    z_recv,
    back_send,
    back_recv,
):
    m = lax.axis_index("modes")
    g = lax.axis_index("grid")
    core = lax.rem(m, 2)
    yy = lax.rem(m // 2, n)
    zz = m // (2 * n)
    left = (m, lax.rem(g + grid_n - 1, grid_n))
    right = (m, lax.rem(g + 1, grid_n))
    flip = 1 - 2 * core
    share = PLANES // n
    y_at = [lax.rem(yy + d, n) for d in range(n)]
    y_peer = [(zz * 2 * n + at * 2 + core, g) for at in y_at]
    y_cross = [(peer[0] + flip, g) for peer in y_peer]
    z_peer = [(lax.rem(zz + d, n) * 2 * n + yy * 2 + core, g) for d in range(n)]
    order = sorted(range(1, n), key=lambda d: -min(d, n - d))
    order_z = sorted(range(1, n), key=lambda d: min(d, n - d))
    started = []

    def remote(src, dst, send_sem, recv_sem, peer):
        copy = pltpu.make_async_remote_copy(
            src_ref=src,
            dst_ref=dst,
            send_sem=send_sem,
            recv_sem=recv_sem,
            device_id=peer,
            device_id_type=MESH,
        )
        started.append(copy)
        return copy

    def to_left(k, src, dst):
        return remote(src, dst, ring_send.at[0, k], ring_recv.at[0, k], left)

    def to_right(k, src, dst):
        return remote(src, dst, ring_send.at[1, k], ring_recv.at[1, k], right)

    barrier = pltpu.get_barrier_semaphore()
    partners = [left, right] + y_cross + y_peer[1:] + z_peer[1:]
    for partner in partners[0:2]:
        pl.semaphore_signal(barrier, inc=1, device_id=partner, device_id_type=MESH)

    loads = [
        pltpu.make_async_copy(u_ref.at[0], raw.at[0:2], load_sem.at[0]),
        pltpu.make_async_copy(v_ref.at[0], raw.at[2:4], load_sem.at[1]),
        pltpu.make_async_copy(pot_ref, raw.at[4], load_sem.at[2]),
        pltpu.make_async_copy(pair_ref, raw.at[5:7], load_sem.at[3]),
    ]
    for load in loads:
        load.start()
    for partner in partners[2:]:
        pl.semaphore_signal(barrier, inc=1, device_id=partner, device_id_type=MESH)
    row = lax.broadcasted_iota(jnp.int32, (ROWS, LANES), 0)
    top = row < 4

    def flat_plane(x):
        return in_plane(x.reshape(-1, ROWS, LANES), weights).reshape(x.shape)

    def depth(ref, z):
        total = COEF[1] * (ref[z - 1] + ref[z + 1])
        for k in range(2, 5):
            total = total + COEF[k] * (ref[z - k] + ref[z + k])
        return total

    for load in loads:
        load.wait()
    for c in range(7):
        for t in range(ROWS):
            rows[c, t * PLANES : (t + 1) * PLANES, :] = raw[c, :, t * LANES : (t + 1) * LANES]
    for c in range(7):
        for z in range(PLANES):
            value = rows[c, pl.ds(z, ROWS, stride=PLANES), :]
            if c < 4:
                wide[0, 8 + z, c] = value
            else:
                pots[4 + z, c - 4] = value

    def near_far(s, k):
        state = wide.at[s]
        near = [to_left(k, state.at[8:12], state.at[16:20]), to_right(k, state.at[12:16], state.at[4:8])]
        far = [to_left(k + 1, state.at[12:16], state.at[20:24]), to_right(k + 1, state.at[8:12], state.at[0:4])]
        return near, far

    start_near, start_far = near_far(0, 0)
    start_pots = [to_left(2, pots.at[4:8], pots.at[12:16]), to_right(2, pots.at[8:12], pots.at[0:4])]
    pl.semaphore_wait(barrier, len(partners))
    for copy in start_near + start_far + start_pots:
        copy.start()
    spread(weights)

    def section(s, arrive, reach, weight):
        def advance(z):
            lap = base[z - 4] + depth(wide.at[s], z)
            k = slope(wide[s, z], lap, pots[z - 4, 0], pots[z - 4, 1], pots[z - 4, 2])
            for c in range(4):
                inner[z - 4, c] = wide[0, z, c] + reach * k[c]
                if 8 <= z < 16:
                    acc[z - 8, c] = (wide[0, z, c] if s == 0 else acc[z - 8, c]) + weight * k[c]

        base[4:12] = flat_plane(wide[s, 8:16])
        for side in (0, 1):
            arrive(side, 0)
            for z in range(8 + 4 * side, 12 + 4 * side):
                advance(z)
        own[...] = flat_plane(inner[4:12])
        base[0:4] = flat_plane(wide[s, 4:8])
        base[12:16] = flat_plane(wide[s, 16:20])
        for side in (0, 1):
            arrive(side, 1)
            for z in range(4 + 12 * side, 8 + 12 * side):
                advance(z)

    def second_slope(z):
        lap = own[z] + depth(inner, z + 4)
        return slope(inner[z + 4], lap, pots[z + 4, 0], pots[z + 4, 1], pots[z + 4, 2])

    def arrive_start(side, is_far):
        (start_far if is_far else start_near)[1 - side].wait_recv()
        if is_far:
            start_pots[1 - side].wait_recv()

    section(0, arrive_start, 0.5 * DT, DT / 6.0)
    near, far = near_far(1, 3)
    for z in range(PLANES):
        k = second_slope(z)
        for c in range(4):
            wide[1, 8 + z, c] = wide[0, 8 + z, c] + (0.5 * DT) * k[c]
            acc[z, c] = acc[z, c] + (DT / 3.0) * k[c]
        if z == 3:
            near[0].start()
    near[1].start()
    far[0].start()
    far[1].start()

    def arrive_second(side, is_far):
        (far if is_far else near)[1 - side].wait_recv()

    section(1, arrive_second, DT, DT / 3.0)
    state = wide.at[2]
    edges = []
    for k, c in ((5, slice(2, 4)), (6, slice(0, 2))):
        edges.append(to_left(k, state.at[8:12, c], state.at[16:20, c]))
        edges.append(to_right(k, state.at[12:16, c], state.at[4:8, c]))
    for z in range(PLANES):
        k = second_slope(z)
        x = [acc[z, c] + (DT / 6.0) * k[c] for c in range(4)]
        for c in range(4):
            wide[2, 8 + z, c] = x[c]
        dense = x[2] * x[2] + x[3] * x[3]
        an_re = x[0] * x[2] + x[1] * x[3]
        an_im = x[1] * x[2] - x[0] * x[3]
        sums[0, z, 0:8] = jnp.where(top, dense, pltpu.roll(an_re, 4, 0))
        sums[1, z, 0:8] = jnp.where(top, pltpu.roll(dense, 4, 0), an_re)
        sums[0, z, 8:12] = an_im[0:4]
        sums[1, z, 8:12] = pltpu.roll(an_im, 4, 0)[0:4]

    def to_owners(lot, src, piece):
        copies = []
        for d in order + [0]:
            planes = pl.ds(y_at[d] * share, share)
            for cross, peer in ((1, y_cross[d]), (0, y_peer[d])):
                if cross or d > 0:
                    half, at = (1 - core, n + d) if cross else (core, d)
                    copies.append(
                        remote(src.at[half, planes], piece.at[at], y_send.at[lot, at], y_recv.at[lot, at], peer)
                    )
        for copy in copies:
            copy.start()
        return copies

    def summed(copies, src, piece):
        total = src[core, pl.ds(yy * share, share)]
        for copy in copies:
            copy.wait_recv()
        for d in range(1, 2 * n):
            total = total + piece[d]
        return total

    def along_z(lot, gather, value):
        gather[0] = value
        copies = []
        for d in order_z:
            copy = remote(gather.at[0], gather.at[d], z_send.at[lot, d], z_recv.at[lot, d], z_peer[d])
            copy.start()
            copies.append(copy)
        return copies

    def gathered(copies, gather):
        for copy in copies:
            copy.wait_recv()
        total = gather[zz]
        for i in range(1, n):
            total = total + gather[lax.rem(zz + n - i, n)]
        return total

    def back(lot, mine, other):
        copies = []
        for d in order + [0]:
            copies.append(remote(mine.at[0], other.at[d], back_send.at[lot, n + d], back_recv.at[lot, n + d], y_cross[d]))
            if d > 0:
                copies.append(remote(mine.at[0], mine.at[d], back_send.at[lot, d], back_recv.at[lot, d], y_peer[d]))
        for copy in copies:
            copy.start()
        return copies

    main_first = to_owners(0, sums, piece_in)
    for copy in edges:
        copy.start()

    own[...] = flat_plane(wide[2, 8:16])
    for comps, copies in ((slice(2, 4), edges[0:2]), (slice(0, 2), edges[2:4])):
        for side in (0, 1):
            copies[1 - side].wait_recv()
            for z in range(4 * side, 4 * side + 4):
                lap = own[z, comps]
                for k in range(1, 5):
                    lap = lap + COEF[k] * (wide[2, 8 + z - k, comps] + wide[2, 8 + z + k, comps])
                own[z, comps] = lap
                if comps.start == 2:
                    kinetic = wide[2, 8 + z, 2] * lap[0] + wide[2, 8 + z, 3] * lap[1]
                    taus[0, z] = kinetic[0:4]
                    taus[1, z] = pltpu.roll(kinetic, 4, 0)[0:4]
        if comps.start == 2:
            tau_first = to_owners(1, taus, tau_piece)
    main_second = along_z(0, gather_in, summed(main_first, sums, piece_in))
    tau_second = along_z(1, tau_gather, summed(tau_first, taus, tau_piece))
    total = gathered(main_second, gather_in)

    rests = []
    for z in range(share):
        dense = (2.0 / modes_total) * total[z, 0:4] + EPS
        an_re = (1.0 / modes_total) * pltpu.roll(total[z, 0:8], 4, 0)[0:4]
        an_im = (1.0 / modes_total) * total[z, 8:12]
        third_root = jnp.exp(jnp.log(dense) * (-1.0 / 3.0))
        fermi = (0.5 * (3.0 * math.pi**2) ** (2.0 / 3.0)) * (dense * third_root)
        an_sq = an_re * an_re + an_im * an_im
        f0 = BETA * fermi - (GAMMA / 3.0) * an_sq * third_root / dense
        f1 = -GAMMA * an_re * third_root
        f2 = -GAMMA * an_im * third_root
        rests.append((0.6 * BETA) * dense * fermi + GAMMA * an_sq * third_root)
        field_mine[0, z, 0:4] = f0
        field_mine[0, z, 4:8] = f1
        field_mine[0, z, 8:12] = f2
    earlier = list(started)
    main_back = back(0, field_mine, field_other)
    tau_total = gathered(tau_second, tau_gather)
    for z in range(share):
        energy_mine[0, z] = (-ALPHA / modes_total) * tau_total[z] + rests[z]
    tau_back = back(1, energy_mine, energy_other)
    for copy in earlier:
        copy.wait_send()
    for copy in main_back:
        copy.wait_recv()

    even = core == 0
    swap = [to_left(7, middle.at[4:8], middle.at[12:16]), to_right(7, middle.at[8:12], middle.at[0:4])]

    def places(z):
        place = z // share
        return lax.rem(yy + n - place, n), z % share

    for z in range(PLANES):
        at, part = places(z)
        mine, other = field_mine[at, part], field_other[at, part]
        lower, upper = jnp.where(even, mine, other), jnp.where(even, other, mine)
        fields = [
            jnp.where(top, lower[0:8], pltpu.roll(upper[0:8], 4, 0)),
            jnp.where(top, pltpu.roll(lower[0:8], 4, 0), upper[0:8]),
            jnp.concatenate([lower[8:12], upper[8:12]], axis=0),
        ]
        k = slope(wide[2, 8 + z], own[z], *fields)
        for c in range(3):
            pots[z + 4, c] = fields[c]
            field_rows[c, z * ROWS : (z + 1) * ROWS, :] = fields[c]
        for c in range(4):
            acc[z, c] = wide[2, 8 + z, c] + (DT / 6.0) * k[c]
            middle[4 + z, c] = wide[2, 8 + z, c] + (0.5 * DT) * k[c]
        if z == 3:
            swap[0].start()
    swap[1].start()
    own[...] = flat_plane(middle[4:12])
    for copy in tau_back:
        copy.wait_recv()
    for copy in main_back + tau_back:
        copy.wait_send()
    for z in range(PLANES):
        at, part = places(z)
        mine, other = energy_mine[at, part], energy_other[at, part]
        lower, upper = jnp.where(even, mine, other), jnp.where(even, other, mine)
        field_rows[3, z * ROWS : (z + 1) * ROWS, :] = jnp.concatenate([lower, upper], axis=0)
    for side in (0, 1):
        swap[1 - side].wait_recv()
        for z in range(4 * side, 4 * side + 4):
            lap = own[z] + depth(middle, z + 4)
            k = slope(middle[4 + z], lap, pots[z + 4, 0], pots[z + 4, 1], pots[z + 4, 2])
            for c in range(4):
                out_rows[c, z * ROWS : (z + 1) * ROWS, :] = acc[z, c] + (DT / 3.0) * k[c]

    for copy in swap:
        copy.wait_send()


def unpack(out_rows, field_rows, uo_ref, vo_ref, fo_ref, outs, sems):
    copies = [
        pltpu.make_async_copy(outs.at[0:4], fo_ref, sems.at[0]),
        pltpu.make_async_copy(outs.at[4:6], uo_ref.at[0], sems.at[1]),
        pltpu.make_async_copy(outs.at[6:8], vo_ref.at[0], sems.at[2]),
    ]
    for c in range(8):
        source = field_rows if c < 4 else out_rows
        for t in range(ROWS):
            outs[c, :, t * LANES : (t + 1) * LANES] = source[c % 4, pl.ds(t, PLANES, stride=ROWS), :]
        if c in (3, 5, 7):
            copies[(c - 3) // 2].start()
    for copy in copies:
        copy.wait()


def solution(mesh):
    modes, grid_n = mesh.shape["modes"], mesh.shape["grid"]
    n = math.isqrt(modes // 2)
    share = PLANES // n
    f32 = jnp.float32
    plane = (ROWS, LANES)
    vmem = pl.BlockSpec(memory_space=pltpu.VMEM)
    hbm = pl.BlockSpec(memory_space=pltpu.HBM)

    def local(u_modes, v_modes, potential, pairing):
        out_rows, field_rows = pl.pallas_call(
            functools.partial(kernel, n, grid_n, float(modes)),
            out_shape=(jax.ShapeDtypeStruct((4, PLANES * ROWS, LANES), f32),) * 2,
            in_specs=[hbm] * 4,
            out_specs=(vmem, vmem),
            scratch_shapes=[
                pltpu.VMEM((7, PLANES, ROWS * LANES), f32),
                pltpu.VMEM((7, PLANES * ROWS, LANES), f32),
                pltpu.VMEM((3, 3 * PLANES, 4) + plane, f32),
                pltpu.VMEM((2 * PLANES, 4) + plane, f32),
                pltpu.VMEM((2 * PLANES, 4) + plane, f32),
                pltpu.VMEM((2 * PLANES, 3) + plane, f32),
                pltpu.VMEM((PLANES, 4) + plane, f32),
                pltpu.VMEM((2 * PLANES, 4) + plane, f32),
                pltpu.VMEM((PLANES, 4) + plane, f32),
                pltpu.VMEM((2, PLANES, 12, LANES), f32),
                pltpu.VMEM((2, PLANES, 4, LANES), f32),
                pltpu.VMEM((2 * n, share, 12, LANES), f32),
                pltpu.VMEM((n, share, 12, LANES), f32),
                pltpu.VMEM((n, share, 12, LANES), f32),
                pltpu.VMEM((n, share, 12, LANES), f32),
                pltpu.VMEM((2 * n, share, 4, LANES), f32),
                pltpu.VMEM((n, share, 4, LANES), f32),
                pltpu.VMEM((n, share, 4, LANES), f32),
                pltpu.VMEM((n, share, 4, LANES), f32),
                pltpu.VMEM((3, 2 * LANES, 2 * LANES), jnp.bfloat16),
                pltpu.SemaphoreType.DMA((4,)),
                pltpu.SemaphoreType.DMA((2, 8)),
                pltpu.SemaphoreType.DMA((2, 8)),
                pltpu.SemaphoreType.DMA((2, 2 * n)),
                pltpu.SemaphoreType.DMA((2, 2 * n)),
                pltpu.SemaphoreType.DMA((2, n)),
                pltpu.SemaphoreType.DMA((2, n)),
                pltpu.SemaphoreType.DMA((2, 2 * n)),
                pltpu.SemaphoreType.DMA((2, 2 * n)),
            ],
            compiler_params=pltpu.CompilerParams(
                collective_id=0, has_side_effects=True, vmem_limit_bytes=16 * 1024 * 1024
            ),
        )(*(pltpu.with_memory_space_constraint(x, pltpu.HBM) for x in (u_modes, v_modes, potential, pairing)))
        return pl.pallas_call(
            unpack,
            out_shape=(
                jax.ShapeDtypeStruct(u_modes.shape, f32),
                jax.ShapeDtypeStruct(v_modes.shape, f32),
                jax.ShapeDtypeStruct((4,) + potential.shape, f32),
            ),
            in_specs=[vmem, vmem],
            out_specs=(hbm, hbm, hbm),
            scratch_shapes=[
                pltpu.VMEM((8, PLANES, ROWS * LANES), f32),
                pltpu.SemaphoreType.DMA((3,)),
            ],
            compiler_params=pltpu.CompilerParams(vmem_limit_bytes=16 * 1024 * 1024),
        )(out_rows, field_rows)

    placed = (
        P("modes", None, "grid", None),
        P("modes", None, "grid", None),
        P("grid", None),
        P(None, "grid", None),
    )
    return jax.shard_map(
        local,
        mesh=mesh,
        in_specs=placed,
        out_specs=(placed[0], placed[1], placed[3]),
        check_vma=False,
    )
```

time: 55.7 us -> 54.2 us (0.973)
  Pallas kernels: 55 us -> 53.4 us
    pallas_call x1, Pallas kernels: 54.2 us -> 52.6 us  [local(): pl.pallas_call(functools.partial(kernel, n, grid_n, float(modes)), out_sh...]
where the time goes in v4:
time: 54.2 us; the launch traced here: 54 us
  Pallas kernels  53.4 us (99%)
  between operations  0.64 us (1%)
    pallas_call x1, Pallas kernels, local(): pl.pallas_call(functools.partial(kernel, n, grid_n, float(modes)), out_sh...  52.6 us

profile of v4, /device:TPU:1, one launch (start us, length us, event | category | flops | bytes accessed | tf_op | source)
XLA Modules:
  0.0 54.0 jit_solution(13545221395945182072)
XLA Ops:
  0.6 52.6 %shard_map.67 = (f32[4,64,128]{2,1,0:T(8,128)S(1)}, f32[4,64,128]{2,1,0:T(8,128)S(1)}) custom-call(f32[1,2,8,1024]{3,2,1,0:T(8,128)} %u_ref.1, f32[1,2,8,1024]{3,2,1,0:T(8,128)} %v_ref.1, f32[8,1024]{1,0:T(8,128)} %pot_ref.1, f32[2,8,1024]{2,1,0:T(8,128)} %pair_ref.1), custom_call_target="tpu_custom_call" | custom-call | tf_op jit(solution)/shard_map/pallas_call | solution.py:432
  53.3 0.7 %shard_map.68 = (f32[1,2,8,1024]{3,2,1,0:T(8,128)}, f32[1,2,8,1024]{3,2,1,0:T(8,128)}, f32[4,8,1024]{2,1,0:T(8,128)}) custom-call(f32[4,64,128]{2,1,0:T(8,128)S(1)} %get-tuple-element.5.out_rows, f32[4,64,128]{2,1,0:T(8,128)S(1)} %get-tuple-element.6.field_rows), custom_call_target="tpu_custom_call" | custom-call | tf_op jit(solution)/shard_map/pallas_call | solution.py:472

commit v5 on v4

--- a/solution.py
+++ b/solution.py
@@ -391,13 +391,26 @@
         mine, other = energy_mine[at, part], energy_other[at, part]
         lower, upper = jnp.where(even, mine, other), jnp.where(even, other, mine)
         field_rows[3, z * ROWS : (z + 1) * ROWS, :] = jnp.concatenate([lower, upper], axis=0)
+    for z in range(PLANES):
+        lap = own[z]
+        for k in range(1, 5):
+            if z - k >= 0:
+                lap = lap + COEF[k] * middle[z + 4 - k]
+            if z + k < PLANES:
+                lap = lap + COEF[k] * middle[z + 4 + k]
+        k = slope(middle[4 + z], lap, pots[z + 4, 0], pots[z + 4, 1], pots[z + 4, 2])
+        for c in range(4):
+            acc[z, c] = acc[z, c] + (DT / 3.0) * k[c]
+    scale = -0.5 * ALPHA * DT / 3.0
     for side in (0, 1):
         swap[1 - side].wait_recv()
         for z in range(4 * side, 4 * side + 4):
-            lap = own[z] + depth(middle, z + 4)
-            k = slope(middle[4 + z], lap, pots[z + 4, 0], pots[z + 4, 1], pots[z + 4, 2])
+            parts = [(scale * COEF[k]) * middle[z + 4 - k] for k in range(1, 5) if z - k < 0]
+            parts += [(scale * COEF[k]) * middle[z + 4 + k] for k in range(1, 5) if z + k >= PLANES]
+            h = sum(parts[1:], parts[0])
+            more = [h[1], -h[0], -h[3], h[2]]
             for c in range(4):
-                out_rows[c, z * ROWS : (z + 1) * ROWS, :] = acc[z, c] + (DT / 3.0) * k[c]
+                out_rows[c, z * ROWS : (z + 1) * ROWS, :] = acc[z, c] + more[c]
 
     for copy in swap:
         copy.wait_send()

time: 54.2 us -> 54.1 us (level)
  no operation moved by 1% of the time
where the time goes in v5:
time: 54.1 us; the launch traced here: 53.9 us
  Pallas kernels  53.3 us (99%)
  between operations  0.64 us (1%)
    pallas_call x1, Pallas kernels, local(): pl.pallas_call(functools.partial(kernel, n, grid_n, float(modes)), out_sh...  52.6 us

profile of v5, /device:TPU:1, one launch (start us, length us, event | category | flops | bytes accessed | tf_op | source)
XLA Modules:
  0.0 53.9 jit_solution(12153936174012160812)
XLA Ops:
  0.6 52.6 %shard_map.67 = (f32[4,64,128]{2,1,0:T(8,128)S(1)}, f32[4,64,128]{2,1,0:T(8,128)S(1)}) custom-call(f32[1,2,8,1024]{3,2,1,0:T(8,128)} %u_ref.1, f32[1,2,8,1024]{3,2,1,0:T(8,128)} %v_ref.1, f32[8,1024]{1,0:T(8,128)} %pot_ref.1, f32[2,8,1024]{2,1,0:T(8,128)} %pair_ref.1), custom_call_target="tpu_custom_call" | custom-call | tf_op jit(solution)/shard_map/pallas_call | solution.py:445
  53.2 0.7 %shard_map.68 = (f32[1,2,8,1024]{3,2,1,0:T(8,128)}, f32[1,2,8,1024]{3,2,1,0:T(8,128)}, f32[4,8,1024]{2,1,0:T(8,128)}) custom-call(f32[4,64,128]{2,1,0:T(8,128)S(1)} %get-tuple-element.5.out_rows, f32[4,64,128]{2,1,0:T(8,128)S(1)} %get-tuple-element.6.field_rows), custom_call_target="tpu_custom_call" | custom-call | tf_op jit(solution)/shard_map/pallas_call | solution.py:485
